TPU v7x, 32 devices: a whole 2x2x4 slice. The times are simulated.
32 devices in a mesh: dp: 4 (over z), atoms: 8 (over y, x, core).
Axes of the slice: x: 2, y: 2, z: 4, core: 2. Of those that a mesh axis runs over, the one named last changes fastest.
Arguments:
- atom_single: bfloat16 [16, 2048, 128], P('dp', 'atoms'), may hold values from -6 to 6
- atom_cond: bfloat16 [16, 2048, 128], P('dp', 'atoms'), may hold values from -6 to 6
- atom_pair: bfloat16 [16, 16, 2048, 128], P('dp', None, 'atoms'), may hold values from -6 to 6
- atom_counts: int32 [16], P('dp'), may hold values from 512 to 2048, as said below
- cotangent: bfloat16 [16, 2048, 128], P('dp', 'atoms'), may hold values from -6 to 6
- first_gain: float32 [128], replicated, may hold values from 0.1 to 1.9
- first_scale: bfloat16 [128, 128], replicated, may hold values from -0.5 to 0.5
- first_lift: float32 [128], replicated, may hold values from -4 to 4
- first_shift: bfloat16 [128, 128], replicated, may hold values from -0.5 to 0.5
- query_weight: bfloat16 [128, 128], replicated, may hold values from -0.5 to 0.5
- query_bias: float32 [128], replicated, may hold values from -3 to 3
- key_weight: bfloat16 [128, 128], replicated, may hold values from -0.5 to 0.5
- value_weight: bfloat16 [128, 128], replicated, may hold values from -0.5 to 0.5
- gate_weight: bfloat16 [128, 128], replicated, may hold values from -0.5 to 0.5
- pair_gain: float32 [16], replicated, may hold values from 0.1 to 1.9
- pair_weight: float32 [16, 4], replicated, may hold values from -1.5 to 1.5
- output_weight: bfloat16 [128, 128], replicated, may hold values from -6 to 6
- branch_gate: bfloat16 [128, 128], replicated, may hold values from -0.5 to 0.5
- branch_lift: float32 [128], replicated, may hold values from -4 to 4
- second_gain: float32 [128], replicated, may hold values from 0.1 to 1.9
- second_scale: bfloat16 [128, 128], replicated, may hold values from -0.5 to 0.5
- second_lift: float32 [128], replicated, may hold values from -4 to 4
- second_shift: bfloat16 [128, 128], replicated, may hold values from -0.5 to 0.5
- hidden_gate: bfloat16 [128, 256], replicated, may hold values from -0.5 to 0.5
- hidden_up: bfloat16 [128, 256], replicated, may hold values from -0.5 to 0.5
- hidden_down: bfloat16 [256, 128], replicated, may hold values from -1 to 1
- closing_gate: bfloat16 [128, 128], replicated, may hold values from -0.5 to 0.5
- closing_lift: float32 [128], replicated, may hold values from -4 to 4
Outputs:
- layer_out: bfloat16 [16, 2048, 128], P('dp', 'atoms')
- atom_grad: float32 [16, 2048, 128], P('dp', 'atoms')
- pair_grad: float32 [16, 16, 2048, 128], P('dp', None, 'atoms')
- cond_grad: float32 [16, 2048, 128], P('dp', 'atoms')
- first_gain_grad: float32 [128], replicated
- first_scale_grad: float32 [128, 128], replicated
- first_lift_grad: float32 [128], replicated
- first_shift_grad: float32 [128, 128], replicated
- query_weight_grad: float32 [128, 128], replicated
- query_bias_grad: float32 [128], replicated
- key_weight_grad: float32 [128, 128], replicated
- value_weight_grad: float32 [128, 128], replicated
- gate_weight_grad: float32 [128, 128], replicated
- pair_gain_grad: float32 [16], replicated
- pair_weight_grad: float32 [16, 4], replicated
- output_weight_grad: float32 [128, 128], replicated
- branch_gate_grad: float32 [128, 128], replicated
- branch_lift_grad: float32 [128], replicated
- second_gain_grad: float32 [128], replicated
- second_scale_grad: float32 [128, 128], replicated
- second_lift_grad: float32 [128], replicated
- second_shift_grad: float32 [128, 128], replicated
- hidden_gate_grad: float32 [128, 256], replicated
- hidden_up_grad: float32 [128, 256], replicated
- hidden_down_grad: float32 [256, 128], replicated
- closing_gate_grad: float32 [128, 128], replicated
- closing_lift_grad: float32 [128], replicated
Inputs may be any that keep to these rules, and one draw needn't show every extreme that they name: `atom_counts`: items are grouped in aligned groups of 4 (one index of dp); in each group one item, drawn from the seed, has all 2048 atoms and another has exactly 512. Atoms at positions at or beyond an item's count are padding.
All inputs are finite; a program needn't handle non-finite values.
Results may differ from a plain program's by a relative error of at most 0.009.
The roundings to bfloat16 on the way count: a program that leaves them out, or rounds other values in their place, can miss the bound.
Values may be sent and summed in bfloat16 or wider, within the bound.
A program may use at most 128 MiB of HBM per device.

v0:
```python
import jax
import jax.numpy as jnp
from jax import lax
from jax.sharding import PartitionSpec as P

QW = 32
KW = 128
HALO = 48


epsilon = 1e-05
masked_score = -1000000000.0
highest = lax.Precision.HIGHEST


def with_halo(value, sides, width):
    for axis, dim in sides:
        peers, length = (lax.axis_size(axis), value.shape[dim])
        up = [(i, (i + 1) % peers) for i in range(peers - 1)]
        down = [(j, i) for i, j in up]
        last = lax.slice_in_dim(value, length - width, length, axis=dim)
        first = lax.slice_in_dim(value, 0, width, axis=dim)
        before = lax.ppermute(last, axis, up)
        after = lax.ppermute(first, axis, down)
        value = jnp.concatenate([before, value, after], axis=dim)
    return value


def matmul(left, right):
    return jnp.dot(left, right, preferred_element_type=jnp.float32)


def outer_rows(left, right):
    return lax.dot_general(
        left, right, (((0,), (0,)), ((), ())), preferred_element_type=jnp.float32
    )


def matmul_back(grads, weight):
    return lax.dot_general(
        grads, weight, (((1,), (1,)), ((), ())), preferred_element_type=jnp.float32
    )


def normalize(values, axis):
    centre = values - jnp.mean(values, axis=axis, keepdims=True)
    inverse = lax.rsqrt(jnp.mean(centre * centre, axis=axis, keepdims=True) + epsilon)
    return (centre * inverse, inverse)


def normalize_back(normed, inverse, grads, axis):
    return inverse * (
        grads
        - jnp.mean(grads, axis=axis, keepdims=True)
        - normed * jnp.mean(grads * normed, axis=axis, keepdims=True)
    )


def adaptive_forward(values, cond_hat, gain, scale_weight, scale_bias, shift_weight):
    values_hat, values_inverse = normalize(values, -1)
    cond_low = (cond_hat * gain).astype(jnp.bfloat16)
    scaling = jax.nn.sigmoid(matmul(cond_low, scale_weight) + scale_bias)
    result = scaling * values_hat + matmul(cond_low, shift_weight)
    return (result.astype(jnp.bfloat16), (values_hat, values_inverse, cond_low, scaling))


def adaptive_back(grads, kept, cond_hat, cond_inverse, gain, scale_weight, shift_weight):
    values_hat, values_inverse, cond_low, scaling = kept
    shift_grad = grads.astype(jnp.bfloat16)
    before_grad = grads * values_hat * scaling * (1.0 - scaling)
    before_low = before_grad.astype(jnp.bfloat16)
    scale_weight_grad = outer_rows(cond_low, before_low)
    scale_bias_grad = jnp.sum(before_grad, axis=0)
    shift_weight_grad = outer_rows(cond_low, shift_grad)
    cond_normed_grad = matmul_back(before_low, scale_weight) + matmul_back(shift_grad, shift_weight)
    gain_grad = jnp.sum(cond_normed_grad * cond_hat, axis=0)
    cond_grad = normalize_back(cond_hat, cond_inverse, cond_normed_grad * gain, -1)
    values_grad = normalize_back(values_hat, values_inverse, grads * scaling, -1)
    return (
        values_grad,
        cond_grad,
        (gain_grad, scale_weight_grad, scale_bias_grad, shift_weight_grad),
    )


def key_windows(extended, windows):
    batch_items, extent, columns = extended.shape
    blocks = extended.reshape(batch_items, extent // QW, QW, columns)
    return jnp.concatenate(
        [blocks[:, offset : offset + windows] for offset in range(KW // QW)], axis=2
    )


def fold_windows(window_grads, windows):
    batch_items, _, _, columns = window_grads.shape
    spread = KW // QW
    summed = jnp.zeros((batch_items, windows + spread - 1, QW, columns), jnp.float32)
    for offset in range(spread):
        summed = summed.at[:, offset : offset + windows].add(
            window_grads[:, :, offset * QW : (offset + 1) * QW]
        )
    return summed.reshape(batch_items, (windows + spread - 1) * QW, columns)


def split_flat(flattened, weight_grads):
    summed = []
    offset = 0
    for member in weight_grads:
        extent = member.size
        summed.append(flattened[offset : offset + extent].reshape(member.shape))
        offset = offset + extent
    return summed


def shards(
    atom_single,
    atom_cond,
    atom_pair,
    atom_counts,
    cotangent,
    first_gain,
    first_scale,
    first_lift,
    first_shift,
    query_weight,
    query_bias,
    key_weight,
    value_weight,
    gate_weight,
    pair_gain,
    pair_weight,
    output_weight,
    branch_gate,
    branch_lift,
    second_gain,
    second_scale,
    second_lift,
    second_shift,
    hidden_gate,
    hidden_up,
    hidden_down,
    closing_gate,
    closing_lift,
):
    batch_items, length, width = atom_single.shape
    heads = pair_weight.shape[1]
    head_dim = width // heads
    windows = length // QW
    rows_all = batch_items * length
    factor = head_dim ** (-0.5)
    anchor = lax.axis_index("atoms") * length
    positions = anchor + jnp.arange(length, dtype=jnp.int32)
    living = (positions[None, :] < atom_counts[:, None]).astype(jnp.float32).reshape(rows_all, 1)
    key_place = (
        anchor
        + QW * jnp.arange(windows, dtype=jnp.int32)[:, None]
        - HALO
        + jnp.arange(KW, dtype=jnp.int32)[None, :]
    )
    key_valid = (key_place[None] >= 0) & (key_place[None] < atom_counts[:, None, None])
    mask_full = key_valid[:, None, :, None, :]
    single = atom_single.reshape(rows_all, width).astype(jnp.float32)
    cond_rows = atom_cond.reshape(rows_all, width)
    cond_hat, cond_inverse = normalize(cond_rows.astype(jnp.float32), -1)
    first_low, first_kept = adaptive_forward(
        single, cond_hat, first_gain, first_scale, first_lift, first_shift
    )
    projection = jnp.concatenate([query_weight, key_weight, value_weight, gate_weight], axis=1)
    projected = matmul(first_low, projection)
    query_low = (projected[:, :width] + query_bias).astype(jnp.bfloat16)
    key_low = projected[:, width : 2 * width].astype(jnp.bfloat16)
    value_low = projected[:, 2 * width : 3 * width].astype(jnp.bfloat16)
    gating = jax.nn.sigmoid(projected[:, 3 * width :])
    pair_hat, pair_inverse = normalize(atom_pair.astype(jnp.float32), 1)
    pair_normed = pair_hat * pair_gain[None, :, None, None]
    pair_term = jnp.einsum("icak,ch->ihak", pair_normed, pair_weight, precision=highest).reshape(
        batch_items, heads, windows, QW, KW
    )
    joined = jnp.concatenate([key_low, value_low], axis=1).reshape(batch_items, length, 2 * width)
    extended = with_halo(joined, (("atoms", 1),), HALO)
    key_value = key_windows(extended, windows)
    key_win = key_value[..., :width].reshape(batch_items, windows, KW, heads, head_dim)
    value_win = key_value[..., width:].reshape(batch_items, windows, KW, heads, head_dim)
    query_win = query_low.reshape(batch_items, windows, QW, heads, head_dim)

    def logits_of():
        scores = (
            jnp.einsum("iwqhd,iwkhd->ihwqk", query_win, key_win, preferred_element_type=jnp.float32)
            * factor
        )
        return jnp.where(mask_full, scores + pair_term, masked_score)

    logits = logits_of()
    highest_logit = jnp.max(logits, axis=-1, keepdims=True)
    log_total = highest_logit + jnp.log(
        jnp.sum(jnp.exp(logits - highest_logit), axis=-1, keepdims=True)
    )
    probs_low = jnp.exp(logits - log_total).astype(jnp.bfloat16)
    attended = jnp.einsum(
        "ihwqk,iwkhd->iwqhd", probs_low, value_win, preferred_element_type=jnp.float32
    ).reshape(rows_all, width)
    gated_low = (gating * attended).astype(jnp.bfloat16)
    branch = matmul(gated_low, output_weight)
    zero_one = jax.nn.sigmoid(matmul(cond_rows, branch_gate) + branch_lift)
    middle = single + living * zero_one * branch
    second_low, second_kept = adaptive_forward(
        middle, cond_hat, second_gain, second_scale, second_lift, second_shift
    )
    gate_pre = matmul(second_low, hidden_gate)
    up_pre = matmul(second_low, hidden_up)
    gate_sig = jax.nn.sigmoid(gate_pre)
    hidden_low = (gate_pre * gate_sig * up_pre).astype(jnp.bfloat16)
    closing = matmul(hidden_low, hidden_down)
    zero_two = jax.nn.sigmoid(matmul(cond_rows, closing_gate) + closing_lift)
    result = middle + living * zero_two * closing
    layer_out = result.astype(jnp.bfloat16).reshape(batch_items, length, width)
    out_grad = cotangent.reshape(rows_all, width).astype(jnp.float32)
    closing_grad = (out_grad * living * zero_two).astype(jnp.bfloat16)
    zero_two_pre = out_grad * living * closing * zero_two * (1.0 - zero_two)
    zero_two_low = zero_two_pre.astype(jnp.bfloat16)
    hidden_down_grad = outer_rows(hidden_low, closing_grad)
    closing_gate_grad = outer_rows(cond_rows, zero_two_low)
    closing_lift_grad = jnp.sum(zero_two_pre, axis=0)
    hidden_grad = matmul_back(closing_grad, hidden_down)
    gate_pre_grad = (hidden_grad * up_pre * gate_sig * (1.0 + gate_pre * (1.0 - gate_sig))).astype(
        jnp.bfloat16
    )
    up_pre_grad = (hidden_grad * gate_pre * gate_sig).astype(jnp.bfloat16)
    hidden_gate_grad = outer_rows(second_low, gate_pre_grad)
    hidden_up_grad = outer_rows(second_low, up_pre_grad)
    second_grad = matmul_back(gate_pre_grad, hidden_gate) + matmul_back(up_pre_grad, hidden_up)
    middle_part, cond_second, second_terms = adaptive_back(
        second_grad, second_kept, cond_hat, cond_inverse, second_gain, second_scale, second_shift
    )
    middle_grad = out_grad + middle_part
    branch_grad = (middle_grad * living * zero_one).astype(jnp.bfloat16)
    zero_one_pre = middle_grad * living * branch * zero_one * (1.0 - zero_one)
    zero_one_low = zero_one_pre.astype(jnp.bfloat16)
    output_weight_grad = outer_rows(gated_low, branch_grad)
    branch_gate_grad = outer_rows(cond_rows, zero_one_low)
    branch_lift_grad = jnp.sum(zero_one_pre, axis=0)
    gated_grad = matmul_back(branch_grad, output_weight)
    attended_low = (gated_grad * gating).astype(jnp.bfloat16)
    gate_low = (gated_grad * attended * gating * (1.0 - gating)).astype(jnp.bfloat16)
    probs = jnp.exp(logits_of() - log_total)
    probs_again = probs.astype(jnp.bfloat16)
    attended_win = attended_low.reshape(batch_items, windows, QW, heads, head_dim)
    probs_grad = jnp.einsum(
        "iwqhd,iwkhd->ihwqk", attended_win, value_win, preferred_element_type=jnp.float32
    )
    value_win_grad = jnp.einsum(
        "ihwqk,iwqhd->iwkhd", probs_again, attended_win, preferred_element_type=jnp.float32
    )
    row_inner = jnp.sum(probs_grad * probs, axis=-1, keepdims=True)
    logits_grad = jnp.where(mask_full, probs * (probs_grad - row_inner), 0.0)
    term_grad = logits_grad.reshape(batch_items, heads, length, KW)
    pair_normed_grad = jnp.einsum("ihak,ch->icak", term_grad, pair_weight, precision=highest)
    pair_weight_grad = jnp.einsum("icak,ihak->ch", pair_normed, term_grad, precision=highest)
    pair_gain_grad = jnp.sum(pair_normed_grad * pair_hat, axis=(0, 2, 3))
    pair_grad = normalize_back(
        pair_hat, pair_inverse, pair_normed_grad * pair_gain[None, :, None, None], 1
    )
    scores_low = logits_grad.astype(jnp.bfloat16)
    query_win_grad = (
        jnp.einsum("ihwqk,iwkhd->iwqhd", scores_low, key_win, preferred_element_type=jnp.float32)
        * factor
    )
    key_win_grad = (
        jnp.einsum("ihwqk,iwqhd->iwkhd", scores_low, query_win, preferred_element_type=jnp.float32)
        * factor
    )
    joined_grad = jnp.concatenate(
        [
            key_win_grad.reshape(batch_items, windows, KW, width),
            value_win_grad.reshape(batch_items, windows, KW, width),
        ],
        axis=3,
    )
    extended_grad = fold_windows(joined_grad, windows)
    rim_grads = jnp.concatenate(
        [extended_grad[:, :HALO], extended_grad[:, HALO + length :]], axis=1
    )
    returned = with_halo(rim_grads.astype(jnp.bfloat16), (("atoms", 1),), HALO).astype(
        rim_grads.dtype
    )
    owned = extended_grad[:, HALO : HALO + length]
    owned = owned.at[:, :HALO].add(returned[:, :HALO])
    owned = owned.at[:, length - HALO :].add(returned[:, 3 * HALO :])
    owned = owned.reshape(rows_all, 2 * width)
    query_full = query_win_grad.reshape(rows_all, width)
    query_bias_grad = jnp.sum(query_full, axis=0)
    projected_grad = jnp.concatenate(
        [query_full.astype(jnp.bfloat16), owned.astype(jnp.bfloat16), gate_low], axis=1
    )
    projection_grad = outer_rows(first_low, projected_grad)
    first_grad = matmul_back(projected_grad, projection)
    single_part, cond_first, first_terms = adaptive_back(
        first_grad, first_kept, cond_hat, cond_inverse, first_gain, first_scale, first_shift
    )
    atom_grad = (middle_grad + single_part).reshape(batch_items, length, width)
    cond_grad = (
        cond_first
        + cond_second
        + matmul_back(zero_one_low, branch_gate)
        + matmul_back(zero_two_low, closing_gate)
    ).reshape(batch_items, length, width)
    weight_grads = [
        first_terms[0],
        first_terms[1],
        first_terms[2],
        first_terms[3],
        projection_grad[:, :width],
        query_bias_grad,
        projection_grad[:, width : 2 * width],
        projection_grad[:, 2 * width : 3 * width],
        projection_grad[:, 3 * width :],
        pair_gain_grad,
        pair_weight_grad,
        output_weight_grad,
        branch_gate_grad,
        branch_lift_grad,
        second_terms[0],
        second_terms[1],
        second_terms[2],
        second_terms[3],
        hidden_gate_grad,
        hidden_up_grad,
        hidden_down_grad,
        closing_gate_grad,
        closing_lift_grad,
    ]
    flattened = jnp.concatenate([member.reshape(-1) for member in weight_grads])
    flattened = lax.psum(flattened, ("dp", "atoms"))
    summed = split_flat(flattened, weight_grads)
    return (
        layer_out,
        atom_grad,
        pair_grad,
        cond_grad,
        summed[0],
        summed[1],
        summed[2],
        summed[3],
        summed[4],
        summed[5],
        summed[6],
        summed[7],
        summed[8],
        summed[9],
        summed[10],
        summed[11],
        summed[12],
        summed[13],
        summed[14],
        summed[15],
        summed[16],
        summed[17],
        summed[18],
        summed[19],
        summed[20],
        summed[21],
        summed[22],
    )


def solution(mesh):
    placed = (
        P("dp", "atoms", None),
        P("dp", "atoms", None),
        P("dp", None, "atoms", None),
        P("dp"),
        P("dp", "atoms", None),
        P(),
        P(),
        P(),
        P(),
        P(),
        P(),
        P(),
        P(),
        P(),
        P(),
        P(),
        P(),
        P(),
        P(),
        P(),
        P(),
        P(),
        P(),
        P(),
        P(),
        P(),
        P(),
        P(),
    )
    return jax.shard_map(
        shards,
        mesh=mesh,
        in_specs=placed,
        out_specs=(
            P("dp", "atoms", None),
            P("dp", "atoms", None),
            P("dp", None, "atoms", None),
            P("dp", "atoms", None),
            P(),
            P(),
            P(),
            P(),
            P(),
            P(),
            P(),
            P(),
            P(),
            P(),
            P(),
            P(),
            P(),
            P(),
            P(),
            P(),
            P(),
            P(),
            P(),
            P(),
            P(),
            P(),
            P(),
        ),
        check_vma=False,
    )
```

profile of v0, /device:TPU:0, one launch (start us, length us, event | category | flops | bytes accessed | tf_op | source)
XLA Modules:
  0.0 378.8 jit_solution(9624744587572545355)
XLA Ops:
  20.2 3.0 collective-permute-start
  24.7 5.8 %convert_reduce_fusion = f32[4,256,128]{2,1,0:T(8,128)S(1)} fusion(bf16[4,16,256,128]{3,2,1,0:T(8,128)(2,1)} %param.42), kind=kLoop, calls=%fused_computation.2 | loop fusion | flops 4063232 | bytes 4718592 | tf_op jit(solution)/shard_map/reduce_sum | solution.py:46
  30.6 4.0 %fusion.11 = f32[4,256,128]{2,1,0:T(8,128)S(1)} fusion(f32[4,256,128]{2,1,0:T(8,128)S(1)} %broadcast_multiply_fusion.2, bf16[4,16,256,128]{3,2,1,0:T(8,128)(2,1)S(1)} %copy-done.2), kind=kLoop, calls=%fused_computation.13 | loop fusion | flops 8257536 | bytes 5242880 | tf_op jit(solution)/shard_map/reduce_sum | solution.py:47
  38.3 6.7 %convolution_bitcast_fusion.7 = f32[4,4,256,128]{3,1,2,0:T(4,128)S(1)} fusion(f32[16,4]{0,1:T(4,128)S(1)} %copy-done.76, f32[16]{0:T(128)S(1)} %copy-done.74, f32[4,256,128]{2,1,0:T(8,128)S(1)} %add_rsqrt_fusion, f32[4,256,128]{2,1,0:T(8,128)S(1)} %broadcast_multiply_fusion.2, bf16[4,16,256,128]{3,2,1,0:T(8,128)(2,1)S(1)} %copy-done.2), kind=kOutput, calls=%fused_computation.44 | convolution fusion | flops 109051904 | bytes 7340352 | tf_op jit(solution)/shard_map/icak,ch->ihak/dot_general | solution.py:176
  52.2 2.7 fusion.131
  58.2 3.0 copy.114
  61.2 3.2 reshape.631
  74.7 2.3 fusion.119
  77.2 2.2 multiply_convert_fusion.4
  81.6 2.7 reshape.633
  86.3 2.4 fusion.54
  88.7 23.2 %fusion.132 = (bf16[4,4,8,32,128]{4,3,2,1,0:T(8,128)(2,1)S(1)}, f32[4,4,8,32,128]{4,3,2,1,0:T(8,128)}) fusion(f32[4,4,8,32,128]{4,3,2,1,0:T(8,128)S(1)} %fusion.57, f32[4,4,8,32,128]{4,3,2,1,0:T(8,128)S(1)} %get-tuple-element.270, f32[4,4,8,32]{3,2,1,0:T(8,128)S(1)} %log_add_fusion, pred[4,8,128]{2,1,0:T(8,128)(4,1)S(1)} %compare_and_fusion), kind=kOutput, calls=%fused_computation.252 | output fusion | flops 3674239 | bytes 7360512 | tf_op jit(solution)/shard_map/sub | solution.py:255
  113.8 2.1 bitcast_convert_fusion
  121.2 3.0 copy.124
  128.6 5.1 %collective-permute-start.2 = (bf16[4,48,256]{2,1,0:T(8,128)(2,1)}, bf16[4,48,256]{2,1,0:T(8,128)(2,1)}, u32[]{:S(2)}, u32[]{:S(2)}) collective-permute-start(bf16[4,48,256]{2,1,0:T(8,128)(2,1)} %get-tuple-element.248), channel_id=1, source_target_pairs={{0,1},{1,2},{2,3},{3,4},{4,5},{5,6},{6,7},{8,9},{9,10},{10,11},{11... | collective-permute-start | bytes 294920 | tf_op jit(solution)/shard_map/ppermute | solution.py:23
  138.2 2.7 reshape.675
  143.4 21.5 %fusion.10 = (f32[16]{0:T(128)}, f32[4,256,128]{2,1,0:T(8,128)}, f32[4,256,128]{2,1,0:T(8,128)}, f32[4,16,256,128]{3,1,2,0:T(8,128)S(1)}, f32[4,256,128,16]{2,3,1,0:T(8,128)}) fusion(f32[4,256,128]{2,1,0:T(8,128)S(1)} %copy-done.17, f32[4,256,128]{2,1,0:T(8,128)S(1)} %copy-done.11, bf16[4,16,256,128]{3,2,1,0:T(8,128)(2,1)} %param.42, f32[16]{0:T(128)S(1)} %copy-done.75, ...), kind=kOutput, calls=%fused_computation.12 | convolution fusion | flops 121372656 | bytes 25166208 | tf_op jit(solution)/shard_map/ihak,ch->icak/dot_general | solution.py:257
  164.8 11.3 %fusion.40 = f32[16,4]{1,0:T(8,128)S(1)} fusion(f32[4,4,256,128]{3,2,1,0:T(8,128)S(1)} %bitcast.226, f32[4,16,256,128]{3,1,2,0:T(8,128)S(1)} %get-tuple-element.209), kind=kOutput, calls=%fused_computation.79 | convolution fusion | flops 100663296 | bytes 10486016 | tf_op jit(solution)/shard_map/icak,ihak->ch/dot_general | solution.py:258
  178.9 7.5 %fusion.9 = f32[4,16,256,128]{3,1,2,0:T(8,128)S(1)} fusion(f32[4,256,128,16]{2,3,1,0:T(8,128)} %get-tuple-element.278, f32[4,256,128]{2,1,0:T(8,128)S(1)} %broadcast_multiply_fusion, f32[4,256,128]{2,1,0:T(8,128)S(1)} %broadcast_multiply_fusion.1, f32[16]{0:T(128)S(1)} %copy-done.75, f32[4,256,128]{2,1,0:T(8,128)S(1)} %copy-done.17, ...), kind=kLoop, calls=%fused_computation.11 | loop fusion | flops 16777216 | bytes 23068736 | tf_op jit(solution)/shard_map/mul | solution.py:52
  186.4 6.0 %copy.134 = f32[4,16,256,128]{3,2,1,0:T(8,128)} copy(f32[4,16,256,128]{3,1,2,0:T(8,128)S(1)} %fusion.9) | data formatting | bytes 16777216
  201.5 26.3 %concatenate.46 = f32[279504]{0:T(1024)} concatenate(f32[128]{0:T(128)S(1)} %get-tuple-element.195, f32[16384]{0:T(1024)S(1)} %convolution_bitcast_fusion.5, f32[128]{0:T(128)} %get-tuple-element.203, f32[16384]{0:T(1024)S(1)} %copy-done.47, f32[16384]{0:T(1024)} %get-tuple-element.261, f32[128]{0:T(128)} %reduce_sum.277, f32[16384]{0:T(1024)} %get-tuple-element.260, ...), dimensions={0} | concatenate | bytes 2236032 | tf_op jit(solution)/shard_map/concatenate | solution.py:332
  227.8 2.1 convolution_add_fusion.1
  232.5 129.8 %all-reduce.3.cloned.1.call-done = f32[279504]{0:T(1024)} async-done(((f32[279504]{0:T(1024)}), f32[279504]{0:T(1024)}) %all-reduce.3.cloned.1.call-update) | async-done | bytes 1118032 | tf_op jit(solution)/shard_map/psum | solution.py:333
  369.5 2.1 slice_bitcast_fusion.1
  (304 shorter events, 82.4 us)
Async XLA Ops:
  7.2 61.9 %copy-start = (bf16[256,128]{1,0:T(8,128)(2,1)S(1)}, bf16[256,128]{1,0:T(8,128)(2,1)}, u32[]{:S(2)}) copy-start(bf16[256,128]{1,0:T(8,128)(2,1)} %param.65) | copy-start | bytes 196612
  7.2 9.6 %copy-start.19 = (bf16[4,256,128]{2,1,0:T(8,128)(2,1)S(1)}, bf16[4,256,128]{2,1,0:T(8,128)(2,1)}, u32[]{:S(2)}) copy-start(bf16[4,256,128]{2,1,0:T(8,128)(2,1)} %param.40) | copy-start | bytes 786436
  7.2 9.6 %copy-start.62 = (bf16[128,128]{1,0:T(8,128)(2,1)S(1)}, bf16[128,128]{1,0:T(8,128)(2,1)}, u32[]{:S(2)}) copy-start(bf16[128,128]{1,0:T(8,128)(2,1)} %param.46) | copy-start | bytes 98308
  7.2 9.6 %copy-start.84 = (f32[128]{0:T(128)S(1)}, f32[128]{0:T(128)}, u32[]{:S(2)}) copy-start(f32[128]{0:T(128)} %param.47) | copy-start | bytes 1540
  7.3 355.0 %all-reduce.3.cloned.1.call-start = ((), (), s32[]{:S(2)}) async-start(), calls=%async_computation | async-start | bytes 2236416 | tf_op jit(solution)/shard_map/psum | solution.py:333
  9.6 8.4 %copy-start.68 = (f32[1,2,4,128]{3,1,2,0:T(2,128)}, f32[1,2,4,128]{3,1,2,0:T(2,128)S(1)}, u32[]{:S(2)}) copy-start(f32[1,2,4,128]{3,1,2,0:T(2,128)S(1)} %copy.145) | copy-start | bytes 12292
  10.9 7.0 %copy-start.70 = (f32[1,2,4,128]{3,1,2,0:T(2,128)}, f32[1,2,4,128]{3,1,2,0:T(2,128)S(1)}, u32[]{:S(2)}) copy-start(f32[1,2,4,128]{3,1,2,0:T(2,128)S(1)} %copy.146) | copy-start | bytes 12292
  11.0 7.0 %copy-start.55 = (bf16[128,128]{1,0:T(8,128)(2,1)S(1)}, bf16[128,128]{1,0:T(8,128)(2,1)}, u32[]{:S(2)}) copy-start(bf16[128,128]{1,0:T(8,128)(2,1)} %param.48) | copy-start | bytes 98308
  16.8 20.4 %copy-start.21 = (bf16[1024,128]{1,0:T(8,128)(2,1)}, bf16[1024,128]{1,0:T(8,128)(2,1)S(1)}, u32[]{:S(2)}) copy-start(bf16[1024,128]{1,0:T(8,128)(2,1)S(1)} %get-tuple-element.256) | copy-start | bytes 786436
  19.3 15.4 %copy-start.12 = (f32[1024,512]{1,0:T(8,128)}, f32[1024,512]{1,0:T(8,128)S(1)}, u32[]{:S(2)}) copy-start(f32[1024,512]{1,0:T(8,128)S(1)} %fusion.133) | copy-start | bytes 6291460
  19.4 11.1 %copy-start.26 = (bf16[1024,256]{1,0:T(8,128)(2,1)}, bf16[1024,256]{1,0:T(8,128)(2,1)S(1)}, u32[]{:S(2)}) copy-start(bf16[1024,256]{1,0:T(8,128)(2,1)S(1)} %slice.491) | copy-start | bytes 1572868
  20.2 27.9 %collective-permute-start = (bf16[4,48,256]{2,1,0:T(8,128)(2,1)}, bf16[4,48,256]{2,1,0:T(8,128)(2,1)}, u32[]{:S(2)}, u32[]{:S(2)}) collective-permute-start(bf16[4,48,256]{2,1,0:T(8,128)(2,1)} %get-tuple-element.254), channel_id=1, source_target_pairs={{0,1},{1,2},{2,3},{3,4},{4,5},{5,6},{6,7},{8,9},{9,10},{10,11},{11... | collective-permute-start | bytes 294920 | tf_op jit(solution)/shard_map/ppermute | solution.py:23
  23.2 24.9 %collective-permute-start.1 = (bf16[4,48,256]{2,1,0:T(8,128)(2,1)}, bf16[4,48,256]{2,1,0:T(8,128)(2,1)}, u32[]{:S(2)}, u32[]{:S(2)}) collective-permute-start(bf16[4,48,256]{2,1,0:T(8,128)(2,1)} %get-tuple-element.255), channel_id=1, source_target_pairs={{1,0},{2,1},{3,2},{4,3},{5,4},{6,5},{7,6},{9,8},{10,9},{11,10},{12... | collective-permute-start | bytes 294920 | tf_op jit(solution)/shard_map/ppermute | solution.py:24
  30.6 7.7 %copy-start.10 = (f32[4,256,128]{2,1,0:T(8,128)}, f32[4,256,128]{2,1,0:T(8,128)S(1)}, u32[]{:S(2)}) copy-start(f32[4,256,128]{2,1,0:T(8,128)S(1)} %broadcast_multiply_fusion.2) | copy-start | bytes 1572868
  88.7 23.2 %copy-start.6 = (bf16[4,8,32,4,32]{4,3,2,1,0:T(4,128)(2,1)S(1)}, bf16[4,8,32,4,32]{4,3,2,1,0:T(4,128)(2,1)}, u32[]{:S(2)}) copy-start(bf16[4,8,32,4,32]{4,3,2,1,0:T(4,128)(2,1)} %reshape.628) | copy-start | bytes 786436
  127.8 8.8 %copy-start.4 = (f32[4,11,32,256]{3,2,1,0:T(8,128)}, f32[4,11,32,256]{3,2,1,0:T(8,128)S(1)}, u32[]{:S(2)}) copy-start(f32[4,11,32,256]{3,2,1,0:T(8,128)S(1)} %fusion.53) | copy-start | bytes 4325380
  128.6 64.1 %collective-permute-start.2 = (bf16[4,48,256]{2,1,0:T(8,128)(2,1)}, bf16[4,48,256]{2,1,0:T(8,128)(2,1)}, u32[]{:S(2)}, u32[]{:S(2)}) collective-permute-start(bf16[4,48,256]{2,1,0:T(8,128)(2,1)} %get-tuple-element.248), channel_id=1, source_target_pairs={{0,1},{1,2},{2,3},{3,4},{4,5},{5,6},{6,7},{8,9},{9,10},{10,11},{11... | collective-permute-start | bytes 294920 | tf_op jit(solution)/shard_map/ppermute | solution.py:23
  133.8 58.9 %collective-permute-start.3 = (bf16[4,48,256]{2,1,0:T(8,128)(2,1)}, bf16[4,48,256]{2,1,0:T(8,128)(2,1)}, u32[]{:S(2)}, u32[]{:S(2)}) collective-permute-start(bf16[4,48,256]{2,1,0:T(8,128)(2,1)} %get-tuple-element.249), channel_id=1, source_target_pairs={{1,0},{2,1},{3,2},{4,3},{5,4},{6,5},{7,6},{9,8},{10,9},{11,10},{12... | collective-permute-start | bytes 294920 | tf_op jit(solution)/shard_map/ppermute | solution.py:24
  186.4 6.3 %copy-start.13 = (f32[4,256,256]{2,1,0:T(8,128)S(1)}, f32[4,256,256]{2,1,0:T(8,128)}, u32[]{:S(2)}) copy-start(f32[4,256,256]{2,1,0:T(8,128)} %slice.393) | copy-start | bytes 3145732
  201.4 26.4 %copy-start.31 = (bf16[1024,128]{1,0:T(8,128)(2,1)S(1)}, bf16[1024,128]{1,0:T(8,128)(2,1)}, u32[]{:S(2)}) copy-start(bf16[1024,128]{1,0:T(8,128)(2,1)} %get-tuple-element.246) | copy-start | bytes 786436
  201.4 26.4 %copy-start.59 = (bf16[128,128]{1,0:T(8,128)(2,1)S(1)}, bf16[128,128]{1,0:T(8,128)(2,1)}, u32[]{:S(2)}) copy-start(bf16[128,128]{1,0:T(8,128)(2,1)} %param.57) | copy-start | bytes 98308
  201.4 26.5 %copy-start.80 = (f32[128]{0:T(128)S(1)}, f32[128]{0:T(128)}, u32[]{:S(2)}) copy-start(f32[128]{0:T(128)} %param.59) | copy-start | bytes 1540
  201.4 26.5 %copy-start.82 = (f32[128]{0:T(128)S(1)}, f32[128]{0:T(128)}, u32[]{:S(2)}) copy-start(f32[128]{0:T(128)} %param.45) | copy-start | bytes 1540
  231.0 140.6 %copy-start.1 = (bf16[256,128]{1,0:T(8,128)(2,1)S(1)}, bf16[256,128]{1,0:T(8,128)(2,1)}, u32[]{:S(2)}) copy-start(bf16[256,128]{1,0:T(8,128)(2,1)} %param.65) | copy-start | bytes 196612
  (71 other events, 190.7 us)
Sparse Core Ops, SparseCore 0:
  227.9 134.3 all-reduce.2
where the time goes:
time: 385 us; the launch traced here: 379 us
  waiting for transfers between devices  130 us (34%)
  matrix products  80.7 us (21%)
  local copies, waits for them, and re-layouts  79.7 us (21%)
  other arithmetic  61.7 us (16%)
  between operations  15.7 us (4%)
  starting transfers between devices  11.1 us (3%)
    psum x1, waiting for transfers between devices, shards(): flattened = lax.psum(flattened, ('dp', 'atoms'))  130 us
    concatenate x1, local copies, waits for them, and re-layouts, shards(): flattened = jnp.concatenate([member.reshape(-1) for member in weight_grads])  26.3 us
    sub x1, other arithmetic, shards(): logits_grad = jnp.where(mask_full, probs * (probs_grad - row_inner), 0.0)  23.2 us
    dot_general x1, matrix products, shards(): jnp.einsum('ihak,ch->icak', term_grad, pair_weight, precision=highest)  21.5 us
    unnamed x192, local copies, waits for them, and re-layouts  13.7 us
    dot_general x11, matrix products, matmul_back(): lax.dot_general(grads, weight, (((1,), (1,)), ((), ())), preferred_elemen...  11.8 us
    dot_general x1, matrix products, shards(): jnp.einsum('icak,ihak->ch', pair_normed, term_grad, precision=highest)  11.3 us
    dot_general x11, matrix products, matmul(): return jnp.dot(left, right, preferred_element_type=jnp.float32)  10.1 us
  transfers between devices with their start and end apart: 5, of which 1 were waited for; matrix products, arithmetic and copies ran while one was open for 22% of the time, Pallas kernels for 0%

commit v1 on v0

v1 whole, which is shorter than its diff:
```python
import functools

import jax
import jax.numpy as jnp
from jax import lax
from jax.experimental import pallas as pl
from jax.experimental.pallas import tpu as pltpu
from jax.sharding import PartitionSpec as P

QW = 32
KW = 128
HALO = 48
SPREAD = KW // QW
EPSILON = 1e-05
MASKED = -1000000000.0
HIGHEST = lax.Precision.HIGHEST
MESH = pl.DeviceIdType.MESH
F32 = jnp.float32
BF16 = jnp.bfloat16

GROUP_ONE = (
    "hidden_gate_a",
    "hidden_gate_b",
    "hidden_up_a",
    "hidden_up_b",
    "hidden_down_a",
    "hidden_down_b",
    "output_weight",
    "branch_gate",
    "closing_gate",
    "second_scale",
    "second_shift",
    "gate_weight",
)
GROUP_TWO = ("query_weight", "key_weight", "value_weight", "first_scale", "first_shift")
VECTORS = (
    "first_gain",
    "first_lift",
    "query_bias",
    "branch_lift",
    "second_gain",
    "second_lift",
    "closing_lift",
)


def mm(a, b, precision=None):
    return lax.dot_general(
        a, b, (((1,), (0,)), ((), ())), precision=precision, preferred_element_type=F32
    )


def mm_t(a, b, precision=None):
    return lax.dot_general(
        a, b, (((1,), (1,)), ((), ())), precision=precision, preferred_element_type=F32
    )


def t_mm(a, b):
    return lax.dot_general(a, b, (((0,), (0,)), ((), ())), preferred_element_type=F32)


def sigmoid(v):
    return 1.0 / (1.0 + jnp.exp(-v))


def lane_mean(v):
    return jnp.mean(v, axis=-1, keepdims=True)


def normalize(v):
    centre = v - lane_mean(v)
    inverse = lax.rsqrt(lane_mean(centre * centre) + EPSILON)
    return centre * inverse, jnp.broadcast_to(inverse, v.shape)


def normalize_back(normed, inverse, grads):
    return inverse * (grads - lane_mean(grads) - normed * lane_mean(grads * normed))


def lanes(*parts):
    return jnp.concatenate(parts, axis=1)


def rows(*parts):
    return jnp.concatenate(parts, axis=0)


def col_sum(v):
    return jnp.sum(v, axis=0, keepdims=True)


def iota(shape, axis):
    return lax.broadcasted_iota(jnp.int32, shape, axis)


def shard_rows(total, peers):
    return -(-total // (16 * peers)) * 16


def main_kernel(
    n_a,
    n_d,
    counts,
    single,
    cond,
    cot,
    pair_hbm,
    first_gain,
    first_scale,
    first_lift,
    first_shift,
    query_weight,
    query_bias,
    key_weight,
    value_weight,
    gate_weight,
    pair_gain,
    pair_weight,
    output_weight,
    branch_gate,
    branch_lift,
    second_gain,
    second_scale,
    second_lift,
    second_shift,
    hidden_gate,
    hidden_up,
    hidden_down,
    closing_gate,
    closing_lift,
    layer_o,
    agrad_o,
    cgrad_o,
    dl_o,
    t_o,
    mean_o,
    wide_o,
    red1_o,
    red2_o,
    pair_s,
    kv_s,
    q_s,
    first_s,
    chat_s,
    cinv_s,
    shat_s,
    sinv_s,
    sig_s,
    gating_s,
    term_s,
    probs_s,
    inv_s,
    mean_s,
    att_s,
    mid_grad_s,
    cnorm_s,
    cdir_s,
    dlow_s,
    glow_s,
    dl_s,
    t_s,
    dq_s,
    kvg_s,
    layer_s,
    agrad_s,
    cgrad_s,
    wide_s,
    widet_s,
    headmask_s,
    pacc_s,
    acc1_s,
    acc2_s,
    halo_send,
    halo_recv,
    send1,
    recv1,
    zall1,
    red1_s,
    send2,
    recv2,
    zall2,
    red2_s,
    pair_sem,
    out_sem,
    misc_sem,
    kv_send_sem,
    kv_recv_sem,
    hg_send_sem,
    hg_recv_sem,
    rs1_send,
    rs1_recv,
    z1_send,
    z1_recv,
    ag1_send,
    ag1_recv,
    rs2_send,
    rs2_recv,
    z2_send,
    z2_recv,
    ag2_send,
    ag2_recv,
):
    items, length, width = single.shape
    windows = length // QW
    channels, heads = pair_weight.shape
    head_dim = width // heads
    factor = head_dim ** (-0.5)
    me = lax.axis_index("atoms")
    me_d = lax.axis_index("dp")
    anchor = me * length
    has_left = me > 0
    has_right = me < n_a - 1

    def pair_copy(i):
        return pltpu.make_async_copy(pair_hbm.at[i], pair_s.at[i], pair_sem.at[i])

    for i in range(items):
        pair_copy(i).start()

    kv_s[:, 0:HALO, :] = jnp.zeros((items, HALO, 2 * width), BF16)
    kv_s[:, HALO + length : 2 * HALO + length, :] = jnp.zeros((items, HALO, 2 * width), BF16)
    halo_recv[...] = jnp.zeros(halo_recv.shape, BF16)

    barrier = pltpu.get_barrier_semaphore()

    def greet_atoms(k, carry):
        pl.semaphore_signal(
            barrier, inc=1, device_id={"atoms": lax.rem(me + k, n_a)}, device_id_type=MESH
        )
        return carry

    def greet_dp(k, carry):
        pl.semaphore_signal(
            barrier, inc=1, device_id={"dp": lax.rem(me_d + k, n_d)}, device_id_type=MESH
        )
        return carry

    lax.fori_loop(1, n_a, greet_atoms, 0)
    lax.fori_loop(1, n_d, greet_dp, 0)

    hq = heads * QW
    cq = channels * QW
    headmask_s[...] = jnp.where(
        iota((hq, width), 0) // QW == iota((hq, width), 1) // head_dim, 1.0, 0.0
    ).astype(BF16)
    pick_head = jnp.where(iota((hq, heads), 0) // QW == iota((hq, heads), 1), 1.0, 0.0)
    weighted = mm_t(pick_head, pair_weight[...], HIGHEST) * pair_gain[...]
    weighted = weighted - lane_mean(weighted)
    spread = jnp.where(iota((channels, cq), 0) == iota((channels, cq), 1) // QW, 1.0, 0.0).astype(
        BF16
    )
    same_row = iota((hq, cq), 0) % QW == iota((hq, cq), 1) % QW
    high = weighted.astype(BF16)
    low = (weighted - high.astype(F32)).astype(BF16)
    wide_high = jnp.where(same_row, mm(high, spread), 0.0)
    wide_low = jnp.where(same_row, mm(low, spread), 0.0)
    wide_s[0:hq, :] = wide_high.astype(BF16)
    wide_s[hq : 2 * hq, :] = wide_low.astype(BF16)
    widet_s[:, 0:hq] = wide_high.T.astype(BF16)
    widet_s[:, hq : 2 * hq] = wide_low.T.astype(BF16)
    pltpu.make_async_copy(widet_s, wide_o, misc_sem.at[0]).start()

    acc1_s[...] = jnp.zeros(acc1_s.shape, F32)
    acc2_s[...] = jnp.zeros(acc2_s.shape, F32)
    pacc_s[...] = jnp.zeros(pacc_s.shape, F32)

    def add1(name, value):
        at = GROUP_ONE.index(name) * width
        acc1_s[at : at + value.shape[0], :] += value

    def add2(name, value):
        at = GROUP_TWO.index(name) * width
        acc2_s[at : at + value.shape[0], :] += value

    vector_at = len(GROUP_TWO) * width

    def add_vector(name, value):
        at = vector_at + VECTORS.index(name)
        acc2_s[at : at + 1, :] += value

    pair_at = vector_at + 8

    def alive(i):
        place = anchor + iota((length, width), 0)
        return jnp.where(place < counts[i], 1.0, 0.0)

    def project(i, carry):
        single_hat, single_inv = normalize(single[i].astype(F32))
        cond_hat, cond_inv = normalize(cond[i].astype(F32))
        low1 = (cond_hat * first_gain[...]).astype(BF16)
        pre = mm(low1, lanes(first_scale[...], first_shift[...]))
        scaling = sigmoid(pre[:, :width] + first_lift[...])
        first = (scaling * single_hat + pre[:, width:]).astype(BF16)
        qkvg = mm(
            first, lanes(query_weight[...], key_weight[...], value_weight[...], gate_weight[...])
        )
        q_s[i] = (qkvg[:, :width] + query_bias[...]).astype(BF16)
        kv_s[i, HALO : HALO + length, :] = qkvg[:, width : 3 * width].astype(BF16)
        gating_s[i] = sigmoid(qkvg[:, 3 * width :])
        first_s[i] = first
        shat_s[i] = single_hat
        sinv_s[i] = single_inv
        chat_s[i] = cond_hat
        cinv_s[i] = cond_inv
        sig_s[i] = scaling
        return carry

    lax.fori_loop(0, items, project, 0)

    pl.semaphore_wait(barrier, n_a - 1 + n_d - 1)

    def kv_right():
        return pltpu.make_async_remote_copy(
            src_ref=kv_s.at[:, pl.ds(length, HALO), :],
            dst_ref=kv_s.at[:, pl.ds(0, HALO), :],
            send_sem=kv_send_sem.at[0],
            recv_sem=kv_recv_sem.at[0],
            device_id={"atoms": lax.rem(me + 1, n_a)},
            device_id_type=MESH,
        )

    def kv_left():
        return pltpu.make_async_remote_copy(
            src_ref=kv_s.at[:, pl.ds(HALO, HALO), :],
            dst_ref=kv_s.at[:, pl.ds(HALO + length, HALO), :],
            send_sem=kv_send_sem.at[1],
            recv_sem=kv_recv_sem.at[1],
            device_id={"atoms": lax.rem(me + n_a - 1, n_a)},
            device_id_type=MESH,
        )

    @pl.when(has_right)
    def _():
        kv_right().start()

    @pl.when(has_left)
    def _():
        kv_left().start()

    def pair_rows(i, w):
        return pair_s[i, :, w * QW : (w + 1) * QW, :]

    def pair_forward(i, carry):
        pair_copy(i).wait()
        wide = wide_s[...]
        for w in range(0, windows, 2):
            invs = []
            for v in (w, w + 1):
                block = pair_rows(i, v).astype(F32)
                mean = jnp.mean(block, axis=0)
                centre = block - mean[None]
                inv = lax.rsqrt(jnp.mean(centre * centre, axis=0) + EPSILON)
                mean_s[i, v * QW : (v + 1) * QW, :] = mean
                inv_s[i, v * QW : (v + 1) * QW, :] = inv
                invs.append(inv)
            both = lanes(pair_rows(i, w).reshape(cq, KW), pair_rows(i, w + 1).reshape(cq, KW))
            product = mm(wide, both)
            product = product[:hq] + product[hq:]
            for v in (0, 1):
                part = product[:, v * KW : (v + 1) * KW].reshape(heads, QW, KW)
                term_s[i, w + v] = (part * invs[v][None]).reshape(hq, KW)
        pltpu.make_async_copy(mean_s.at[i], mean_o.at[i], out_sem.at[0, i]).start()
        return carry

    lax.fori_loop(0, items, pair_forward, 0)

    @pl.when(has_right)
    def _():
        kv_right().wait_send()

    @pl.when(has_left)
    def _():
        kv_left().wait_send()

    @pl.when(has_left)
    def _():
        kv_right().wait_recv()

    @pl.when(has_right)
    def _():
        kv_left().wait_recv()

    def spread_heads(block):
        return rows(*([block] * heads)) * headmask_s[...]

    def gather_heads(wide_block):
        lane = iota((QW, width), 1)
        result = wide_block[(heads - 1) * QW :]
        for h in range(heads - 2, -1, -1):
            result = jnp.where(
                lane < (h + 1) * head_dim, wide_block[h * QW : (h + 1) * QW], result
            )
        return result

    def window_rows(w):
        return slice(w * QW, (w + 1) * QW)

    def keys_of(i, w):
        return kv_s[i, w * QW : w * QW + KW, 0:width]

    def values_of(i, w):
        return kv_s[i, w * QW : w * QW + KW, width : 2 * width]

    def attend(i, carry):
        count = counts[i]
        scores = [
            mm_t(spread_heads(q_s[i, window_rows(w), :]), keys_of(i, w)) for w in range(windows)
        ]
        logits = []
        for w in range(windows):
            place = anchor + (w * QW - HALO) + iota((1, KW), 1)
            valid = (place >= 0) & (place < count)
            logits.append(jnp.where(valid, scores[w] * factor + term_s[i, w], MASKED))
        tops = [jnp.max(v, axis=-1, keepdims=True) for v in logits]
        raised = [jnp.exp(v - top) for v, top in zip(logits, tops)]
        totals = [jnp.sum(v, axis=-1, keepdims=True) for v in raised]
        for w in range(windows):
            probs = raised[w] * (1.0 / totals[w])
            probs_s[i, w] = probs
            attended = mm(probs.astype(BF16), values_of(i, w))
            att_s[i, window_rows(w), :] = gather_heads(attended)
        return carry

    lax.fori_loop(0, items, attend, 0)

    def middle(i, carry):
        live = alive(i)
        att = att_s[i]
        gating = gating_s[i]
        cond_hat = chat_s[i]
        cond_rows = cond[i]
        gated = (gating * att).astype(BF16)
        branch = mm(gated, output_weight[...])
        zeros = mm(cond_rows, lanes(branch_gate[...], closing_gate[...]))
        zero_one = sigmoid(zeros[:, :width] + branch_lift[...])
        zero_two = sigmoid(zeros[:, width:] + closing_lift[...])
        mid = single[i].astype(F32) + live * zero_one * branch
        mid_hat, mid_inv = normalize(mid)
        low2 = (cond_hat * second_gain[...]).astype(BF16)
        scale_shift = lanes(second_scale[...], second_shift[...])
        pre = mm(low2, scale_shift)
        scaling = sigmoid(pre[:, :width] + second_lift[...])
        second = (scaling * mid_hat + pre[:, width:]).astype(BF16)
        gate_up = lanes(hidden_gate[...], hidden_up[...])
        pre2 = mm(second, gate_up)
        inner = hidden_gate.shape[1]
        gate_pre, up_pre = pre2[:, :inner], pre2[:, inner:]
        gate_sig = sigmoid(gate_pre)
        hidden = (gate_pre * gate_sig * up_pre).astype(BF16)
        closing = mm(hidden, hidden_down[...])
        layer_s[i] = (mid + live * zero_two * closing).astype(BF16)
        out_grad = cot[i].astype(F32)
        closing_grad = (out_grad * live * zero_two).astype(BF16)
        zero_two_pre = out_grad * live * closing * zero_two * (1.0 - zero_two)
        zero_two_low = zero_two_pre.astype(BF16)
        down_grad = t_mm(hidden, closing_grad)
        add1("hidden_down_a", down_grad)
        add_vector("closing_lift", col_sum(zero_two_pre))
        hidden_grad = mm_t(closing_grad, hidden_down[...])
        gate_pre_grad = (
            hidden_grad * up_pre * gate_sig * (1.0 + gate_pre * (1.0 - gate_sig))
        ).astype(BF16)
        up_pre_grad = (hidden_grad * gate_pre * gate_sig).astype(BF16)
        gate_up_grad = lanes(gate_pre_grad, up_pre_grad)
        wide_grad = t_mm(second, gate_up_grad)
        for k, name in enumerate(GROUP_ONE[:4]):
            add1(name, wide_grad[:, k * width : (k + 1) * width])
        second_grad = mm_t(gate_up_grad, gate_up)
        before = second_grad * mid_hat * scaling * (1.0 - scaling)
        both = lanes(before.astype(BF16), second_grad.astype(BF16))
        both_grad = t_mm(low2, both)
        add1("second_scale", both_grad[:, :width])
        add1("second_shift", both_grad[:, width:])
        add_vector("second_lift", col_sum(before))
        cond_normed = mm_t(both, scale_shift)
        add_vector("second_gain", col_sum(cond_normed * cond_hat))
        cnorm_s[i] = cond_normed * second_gain[...]
        mid_grad = out_grad + normalize_back(mid_hat, mid_inv, second_grad * scaling)
        mid_grad_s[i] = mid_grad
        branch_grad = (mid_grad * live * zero_one).astype(BF16)
        zero_one_pre = mid_grad * live * branch * zero_one * (1.0 - zero_one)
        add_vector("branch_lift", col_sum(zero_one_pre))
        zero_grads = lanes(zero_one_pre.astype(BF16), zero_two_low)
        gate_grads = t_mm(cond_rows, zero_grads)
        add1("branch_gate", gate_grads[:, :width])
        add1("closing_gate", gate_grads[:, width:])
        cdir_s[i] = mm_t(zero_grads, lanes(branch_gate[...], closing_gate[...]))
        add1("output_weight", t_mm(gated, branch_grad))
        gated_grad = mm_t(branch_grad, output_weight[...])
        dlow_s[i] = (gated_grad * gating).astype(BF16)
        gate_low = (gated_grad * att * gating * (1.0 - gating)).astype(BF16)
        glow_s[i] = gate_low
        add1("gate_weight", t_mm(first_s[i], gate_low))
        pltpu.make_async_copy(layer_s.at[i], layer_o.at[i], out_sem.at[1, i]).start()
        return carry

    lax.fori_loop(0, items, middle, 0)

    class Sum:
        def __init__(self, acc, send, recv, zall, red, sems):
            self.acc, self.send, self.recv, self.zall, self.red = acc, send, recv, zall, red
            self.rs_send, self.rs_recv, self.z_send, self.z_recv, self.ag_send, self.ag_recv = sems
            self.shard = send.shape[1]

        def scatter_copy(self, to, at):
            return pltpu.make_async_remote_copy(
                src_ref=self.send.at[to],
                dst_ref=self.recv.at[at],
                send_sem=self.rs_send.at[to],
                recv_sem=self.rs_recv.at[at],
                device_id={"atoms": to},
                device_id_type=MESH,
            )

        def dp_copy(self, to, at):
            return pltpu.make_async_remote_copy(
                src_ref=self.zall.at[me_d],
                dst_ref=self.zall.at[at],
                send_sem=self.z_send.at[to],
                recv_sem=self.z_recv.at[at],
                device_id={"dp": to},
                device_id_type=MESH,
            )

        def gather_copy(self, to, at):
            return pltpu.make_async_remote_copy(
                src_ref=self.red.at[me],
                dst_ref=self.red.at[at],
                send_sem=self.ag_send.at[to],
                recv_sem=self.ag_recv.at[at],
                device_id={"atoms": to},
                device_id_type=MESH,
            )

        def scatter(self):
            self.send[...] = self.acc[...].astype(BF16).reshape(self.send.shape)

            def go(k, carry):
                self.scatter_copy(lax.rem(me + k, n_a), me).start()
                return carry

            lax.fori_loop(1, n_a, go, 0)

        def over_dp(self):
            start = pl.multiple_of(me * self.shard, 16)
            total = self.acc[pl.ds(start, self.shard), :]
            for k in range(1, n_a):
                peer = lax.rem(me + k, n_a)
                self.scatter_copy(peer, peer).wait_recv()
                total = total + self.recv[peer].astype(F32)
            self.zall[me_d] = total.astype(BF16)

            def go(k, carry):
                self.dp_copy(lax.rem(me_d + k, n_d), me_d).start()
                return carry

            lax.fori_loop(1, n_d, go, 0)

        def gather(self):
            def come(k, carry):
                peer = lax.rem(me_d + k, n_d)
                self.dp_copy(peer, peer).wait_recv()
                return carry

            lax.fori_loop(1, n_d, come, 0)
            total = self.zall[0].astype(F32)
            for d in range(1, n_d):
                total = total + self.zall[d].astype(F32)
            self.red[me] = total.astype(BF16)

            def go(k, carry):
                self.gather_copy(lax.rem(me + k, n_a), me).start()
                return carry

            lax.fori_loop(1, n_a, go, 0)

        def finish(self):
            def end(k, carry):
                peer = lax.rem(me + k, n_a)
                self.gather_copy(peer, peer).wait_recv()
                self.gather_copy(peer, peer).wait_send()
                self.scatter_copy(peer, peer).wait_send()
                return carry

            lax.fori_loop(1, n_a, end, 0)

            def end_dp(k, carry):
                peer = lax.rem(me_d + k, n_d)
                self.dp_copy(peer, peer).wait_send()
                return carry

            lax.fori_loop(1, n_d, end_dp, 0)

    sum1 = Sum(
        acc1_s,
        send1,
        recv1,
        zall1,
        red1_s,
        (rs1_send, rs1_recv, z1_send, z1_recv, ag1_send, ag1_recv),
    )
    sum2 = Sum(
        acc2_s,
        send2,
        recv2,
        zall2,
        red2_s,
        (rs2_send, rs2_recv, z2_send, z2_recv, ag2_send, ag2_recv),
    )
    sum1.scatter()

    def halo_right(i):
        return pltpu.make_async_remote_copy(
            src_ref=halo_send.at[i, 1],
            dst_ref=halo_recv.at[i, 0],
            send_sem=hg_send_sem.at[i, 1],
            recv_sem=hg_recv_sem.at[i, 0],
            device_id={"atoms": lax.rem(me + 1, n_a)},
            device_id_type=MESH,
        )

    def halo_left(i):
        return pltpu.make_async_remote_copy(
            src_ref=halo_send.at[i, 0],
            dst_ref=halo_recv.at[i, 1],
            send_sem=hg_send_sem.at[i, 0],
            recv_sem=hg_recv_sem.at[i, 1],
            device_id={"atoms": lax.rem(me + n_a - 1, n_a)},
            device_id_type=MESH,
        )

    def attend_back(i, carry):
        wide_grads = [spread_heads(dlow_s[i, window_rows(w), :]) for w in range(windows)]
        probs_grads = [mm_t(wide_grads[w], values_of(i, w)) for w in range(windows)]
        inners = [
            jnp.sum(probs_grads[w] * probs_s[i, w], axis=-1, keepdims=True) for w in range(windows)
        ]
        value_parts = [t_mm(probs_s[i, w].astype(BF16), wide_grads[w]) for w in range(windows)]
        key_parts = []
        for w in range(windows):
            logits_grad = probs_s[i, w] * (probs_grads[w] - inners[w])
            low = logits_grad.astype(BF16)
            dq_s[i, window_rows(w), :] = gather_heads(mm(low, keys_of(i, w))) * factor
            key_parts.append(t_mm(low, spread_heads(q_s[i, window_rows(w), :])) * factor)
            inv = inv_s[i, window_rows(w), :]
            by_head = logits_grad.reshape(heads, QW, KW)
            dl_s[i, w] = (by_head * inv[None]).astype(BF16).reshape(hq, KW)
            inner = jnp.sum(by_head * term_s[i, w].reshape(heads, QW, KW), axis=0)
            t_s[i, window_rows(w), :] = inner * inv * inv * (1.0 / channels)
        for part, at in ((key_parts, 0), (value_parts, width)):
            for b in range(windows + SPREAD - 1):
                block = None
                for w in range(max(0, b - SPREAD + 1), min(windows - 1, b) + 1):
                    piece = part[w][(b - w) * QW : (b - w + 1) * QW]
                    block = piece if block is None else block + piece
                kvg_s[i, b * QW : (b + 1) * QW, at : at + width] = block
        halo_send[i, 0] = kvg_s[i, 0:HALO, :].astype(BF16)
        halo_send[i, 1] = kvg_s[i, HALO + length : 2 * HALO + length, :].astype(BF16)

        @pl.when(has_right)
        def _():
            halo_right(i).start()

        @pl.when(has_left)
        def _():
            halo_left(i).start()

        pair_all = lanes(*[pair_rows(i, w).reshape(cq, KW) for w in range(windows)])
        grads_all = lanes(*[dl_s[i, w] for w in range(windows)])
        pacc_s[...] += mm_t(pair_all, grads_all)
        pltpu.make_async_copy(dl_s.at[i], dl_o.at[i], out_sem.at[2, i]).start()
        pltpu.make_async_copy(t_s.at[i], t_o.at[i], out_sem.at[3, i]).start()
        return carry

    lax.fori_loop(0, items, attend_back, 0)
    sum1.over_dp()

    diagonal = jnp.where(iota((cq, hq), 0) % QW == iota((cq, hq), 1) % QW, pacc_s[...], 0.0)
    by_channel = jnp.sum(diagonal.reshape(channels, QW, hq), axis=1)
    fold = jnp.where(iota((hq, width), 0) // QW == iota((hq, width), 1), 1.0, 0.0)
    pair_sums = mm(by_channel, fold, HIGHEST)
    acc2_s[pair_at : pair_at + channels, :] = pair_sums - jnp.mean(
        pair_sums, axis=0, keepdims=True
    )

    def finish_rows(i, carry):
        @pl.when(has_left)
        def _():
            halo_right(i).wait_recv()

        @pl.when(has_right)
        def _():
            halo_left(i).wait_recv()

        kvg_s[i, HALO : 2 * HALO, :] += halo_recv[i, 0].astype(F32)
        kvg_s[i, length : length + HALO, :] += halo_recv[i, 1].astype(F32)
        dq = dq_s[i]
        add_vector("query_bias", col_sum(dq))
        grads = lanes(
            dq.astype(BF16), kvg_s[i, HALO : HALO + length, :].astype(BF16), glow_s[i]
        )
        first = first_s[i]
        weight_grads = t_mm(first, grads[:, : 3 * width])
        for k, name in enumerate(GROUP_TWO[:3]):
            add2(name, weight_grads[:, k * width : (k + 1) * width])
        first_grad = mm_t(
            grads, lanes(query_weight[...], key_weight[...], value_weight[...], gate_weight[...])
        )
        scaling = sig_s[i]
        single_hat = shat_s[i]
        cond_hat = chat_s[i]
        before = first_grad * single_hat * scaling * (1.0 - scaling)
        both = lanes(before.astype(BF16), first_grad.astype(BF16))
        low1 = (cond_hat * first_gain[...]).astype(BF16)
        both_grad = t_mm(low1, both)
        add2("first_scale", both_grad[:, :width])
        add2("first_shift", both_grad[:, width:])
        add_vector("first_lift", col_sum(before))
        cond_normed = mm_t(both, lanes(first_scale[...], first_shift[...]))
        add_vector("first_gain", col_sum(cond_normed * cond_hat))
        agrad_s[i] = mid_grad_s[i] + normalize_back(single_hat, sinv_s[i], first_grad * scaling)
        cond_grad = cond_normed * first_gain[...] + cnorm_s[i]
        cgrad_s[i] = normalize_back(cond_hat, cinv_s[i], cond_grad) + cdir_s[i]
        pltpu.make_async_copy(agrad_s.at[i], agrad_o.at[i], out_sem.at[4, i]).start()
        pltpu.make_async_copy(cgrad_s.at[i], cgrad_o.at[i], out_sem.at[5, i]).start()
        return carry

    lax.fori_loop(0, items, finish_rows, 0)
    sum2.scatter()
    sum1.gather()
    sum2.over_dp()
    sum2.gather()
    sum1.finish()
    red1_out = pltpu.make_async_copy(red1_s, red1_o, misc_sem.at[1])
    red1_out.start()
    sum2.finish()
    red2_out = pltpu.make_async_copy(red2_s, red2_o, misc_sem.at[2])
    red2_out.start()

    def drain(i, carry):
        pltpu.make_async_copy(mean_s.at[i], mean_o.at[i], out_sem.at[0, i]).wait()
        pltpu.make_async_copy(layer_s.at[i], layer_o.at[i], out_sem.at[1, i]).wait()
        pltpu.make_async_copy(dl_s.at[i], dl_o.at[i], out_sem.at[2, i]).wait()
        pltpu.make_async_copy(t_s.at[i], t_o.at[i], out_sem.at[3, i]).wait()
        pltpu.make_async_copy(agrad_s.at[i], agrad_o.at[i], out_sem.at[4, i]).wait()
        pltpu.make_async_copy(cgrad_s.at[i], cgrad_o.at[i], out_sem.at[5, i]).wait()

        @pl.when(has_right)
        def _():
            halo_right(i).wait_send()

        @pl.when(has_left)
        def _():
            halo_left(i).wait_send()

        return carry

    lax.fori_loop(0, items, drain, 0)
    pltpu.make_async_copy(widet_s, wide_o, misc_sem.at[0]).wait()
    red1_out.wait()
    red2_out.wait()


GRADS = (
    "first_gain",
    "first_scale",
    "first_lift",
    "first_shift",
    "query_weight",
    "query_bias",
    "key_weight",
    "value_weight",
    "gate_weight",
    "pair_gain",
    "pair_weight",
    "output_weight",
    "branch_gate",
    "branch_lift",
    "second_gain",
    "second_scale",
    "second_lift",
    "second_shift",
    "hidden_gate",
    "hidden_up",
    "hidden_down",
    "closing_gate",
    "closing_lift",
)
SPLIT = {
    "hidden_gate": ("hidden_gate_a", "hidden_gate_b"),
    "hidden_up": ("hidden_up_a", "hidden_up_b"),
}


def pair_kernel(
    steps,
    pair,
    dl,
    t,
    mean,
    wide,
    red1,
    red2,
    pair_gain,
    pair_weight,
    layer_in,
    agrad_in,
    cgrad_in,
    pgrad,
    layer_o,
    agrad_o,
    cgrad_o,
    *rest,
):
    grads = dict(zip(GRADS, rest[: len(GRADS)]))
    (sem,) = rest[len(GRADS) :]
    step = pl.program_id(0)
    copies = [
        pltpu.make_async_copy(layer_in, layer_o, sem.at[0]),
        pltpu.make_async_copy(agrad_in, agrad_o, sem.at[1]),
        pltpu.make_async_copy(cgrad_in, cgrad_o, sem.at[2]),
    ]

    @pl.when(step == 0)
    def _():
        for copy in copies:
            copy.start()
        width = red1.shape[1]

        def one(name):
            at = GROUP_ONE.index(name) * width
            return red1[at : at + width, :].astype(F32)

        vector_at = len(GROUP_TWO) * width
        tail = red2[vector_at : vector_at + 32, :].astype(F32)
        for name in GRADS:
            ref = grads[name]
            if name in SPLIT:
                for k, part in enumerate(SPLIT[name]):
                    ref[:, k * width : (k + 1) * width] = one(part)
            elif name == "hidden_down":
                ref[0:width, :] = one("hidden_down_a")
                ref[width : 2 * width, :] = one("hidden_down_b")
            elif name in GROUP_ONE:
                ref[...] = one(name)
            elif name in GROUP_TWO:
                at = GROUP_TWO.index(name) * width
                ref[...] = red2[at : at + width, :].astype(F32)
            elif name in VECTORS:
                at = VECTORS.index(name)
                ref[...] = tail[at : at + 1, :]
        channels, heads = pair_weight.shape
        sums = tail[8 : 8 + channels, 0:heads]
        eye = jnp.where(
            iota((channels, channels), 0) == iota((channels, channels), 1), 1.0, 0.0
        )
        gain_column = jnp.sum(eye * pair_gain[...], axis=1, keepdims=True)
        grads["pair_weight"][...] = gain_column * sums
        gain_grad = jnp.sum(pair_weight[...] * sums, axis=1, keepdims=True)
        grads["pair_gain"][...] = jnp.sum(eye * gain_grad, axis=0, keepdims=True)

    channels, span, _ = pair.shape[1:]
    wide_v = wide[...]
    for w in range(0, span // QW, 2):
        both = lanes(dl[0, w], dl[0, w + 1])
        product = mm(wide_v, rows(both, both))
        for v in (0, 1):
            at = slice((w + v) * QW, (w + v + 1) * QW)
            block = pair[0, :, at, :].astype(F32)
            part = product[:, v * KW : (v + 1) * KW].reshape(channels, QW, KW)
            pgrad[0, :, at, :] = part - (block - mean[0, at, :][None]) * t[0, at, :][None]

    @pl.when(step == steps - 1)
    def _():
        for copy in copies:
            copy.wait()


def shards(
    n_a,
    n_d,
    atom_single,
    atom_cond,
    atom_pair,
    atom_counts,
    cotangent,
    *params,
):
    items, length, width = atom_single.shape
    windows = length // QW
    channels = atom_pair.shape[1]
    named = dict(zip(GRADS, params))
    flat = [v.reshape(1, -1) if v.ndim == 1 else v for v in params]
    heads = named["pair_weight"].shape[1]
    hq, cq = heads * QW, channels * QW
    rows1 = len(GROUP_ONE) * width
    rows2 = len(GROUP_TWO) * width + 8 + channels
    shard1, shard2 = shard_rows(rows1, n_a), shard_rows(rows2, n_a)

    vmem = pl.BlockSpec(memory_space=pltpu.VMEM)
    anywhere = pl.BlockSpec(memory_space=pl.ANY)
    by_rows = (items, length, width)
    by_keys = (items, length, KW)
    ext = length + 2 * HALO
    dma = pltpu.SemaphoreType.DMA

    def sds(shape, dtype):
        return jax.ShapeDtypeStruct(shape, dtype)

    outs = pl.pallas_call(
        functools.partial(main_kernel, n_a, n_d),
        out_shape=[
            sds(by_rows, BF16),
            sds(by_rows, F32),
            sds(by_rows, F32),
            sds((items, windows, hq, KW), BF16),
            sds(by_keys, F32),
            sds(by_keys, F32),
            sds((cq, 2 * hq), BF16),
            sds((n_a, shard1, width), BF16),
            sds((n_a, shard2, width), BF16),
        ],
        in_specs=[pl.BlockSpec(memory_space=pltpu.SMEM), vmem, vmem, vmem, anywhere]
        + [vmem] * len(flat),
        out_specs=[anywhere] * 9,
        scratch_shapes=[
            pltpu.VMEM((items, channels, length, KW), BF16),
            pltpu.VMEM((items, ext, 2 * width), BF16),
            pltpu.VMEM(by_rows, BF16),
            pltpu.VMEM(by_rows, BF16),
            pltpu.VMEM(by_rows, F32),
            pltpu.VMEM(by_rows, F32),
            pltpu.VMEM(by_rows, F32),
            pltpu.VMEM(by_rows, F32),
            pltpu.VMEM(by_rows, F32),
            pltpu.VMEM(by_rows, F32),
            pltpu.VMEM((items, windows, hq, KW), F32),
            pltpu.VMEM((items, windows, hq, KW), F32),
            pltpu.VMEM(by_keys, F32),
            pltpu.VMEM(by_keys, F32),
            pltpu.VMEM(by_rows, F32),
            pltpu.VMEM(by_rows, F32),
            pltpu.VMEM(by_rows, F32),
            pltpu.VMEM(by_rows, F32),
            pltpu.VMEM(by_rows, BF16),
            pltpu.VMEM(by_rows, BF16),
            pltpu.VMEM((items, windows, hq, KW), BF16),
            pltpu.VMEM(by_keys, F32),
            pltpu.VMEM(by_rows, F32),
            pltpu.VMEM((items, ext, 2 * width), F32),
            pltpu.VMEM(by_rows, BF16),
            pltpu.VMEM(by_rows, F32),
            pltpu.VMEM(by_rows, F32),
            pltpu.VMEM((2 * hq, cq), BF16),
            pltpu.VMEM((cq, 2 * hq), BF16),
            pltpu.VMEM((hq, width), BF16),
            pltpu.VMEM((cq, hq), F32),
            pltpu.VMEM((n_a * shard1, width), F32),
            pltpu.VMEM((n_a * shard2, width), F32),
            pltpu.VMEM((items, 2, HALO, 2 * width), BF16),
            pltpu.VMEM((items, 2, HALO, 2 * width), BF16),
            pltpu.VMEM((n_a, shard1, width), BF16),
            pltpu.VMEM((n_a, shard1, width), BF16),
            pltpu.VMEM((n_d, shard1, width), BF16),
            pltpu.VMEM((n_a, shard1, width), BF16),
            pltpu.VMEM((n_a, shard2, width), BF16),
            pltpu.VMEM((n_a, shard2, width), BF16),
            pltpu.VMEM((n_d, shard2, width), BF16),
            pltpu.VMEM((n_a, shard2, width), BF16),
            dma((items,)),
            dma((6, items)),
            dma((3,)),
            dma((2,)),
            dma((2,)),
            dma((items, 2)),
            dma((items, 2)),
            dma((n_a,)),
            dma((n_a,)),
            dma((n_d,)),
            dma((n_d,)),
            dma((n_a,)),
            dma((n_a,)),
            dma((n_a,)),
            dma((n_a,)),
            dma((n_d,)),
            dma((n_d,)),
            dma((n_a,)),
            dma((n_a,)),
        ],
        compiler_params=pltpu.CompilerParams(
            collective_id=0, has_side_effects=True, vmem_limit_bytes=56 * 1024 * 1024
        ),
        name="block",
    )(atom_counts, atom_single, atom_cond, cotangent, atom_pair, *flat)
    layer, agrad, cgrad, dl, t, mean, wide, red1, red2 = outs

    parts = 2 if windows % 4 == 0 else 1
    span = length // parts
    steps = items * parts

    def whole(shape):
        return pl.BlockSpec(shape, lambda s: (0,) * len(shape))

    grad_shapes = [
        (1, v.shape[0]) if v.ndim == 1 else v.shape for v in (named[name] for name in GRADS)
    ]
    red1 = red1.reshape(n_a * shard1, width)
    red2 = red2.reshape(n_a * shard2, width)
    pair_spec = pl.BlockSpec((1, channels, span, KW), lambda s: (s // parts, 0, s % parts, 0))
    rows_spec = pl.BlockSpec((1, span, KW), lambda s: (s // parts, s % parts, 0))
    finals = pl.pallas_call(
        functools.partial(pair_kernel, steps),
        grid=(steps,),
        out_shape=[
            sds(atom_pair.shape, F32),
            sds(by_rows, BF16),
            sds(by_rows, F32),
            sds(by_rows, F32),
        ]
        + [sds(shape, F32) for shape in grad_shapes],
        in_specs=[
            pair_spec,
            pl.BlockSpec((1, span // QW, hq, KW), lambda s: (s // parts, s % parts, 0, 0)),
            rows_spec,
            rows_spec,
            whole(wide.shape),
            whole(red1.shape),
            whole(red2.shape),
            whole((1, channels)),
            whole((channels, heads)),
            anywhere,
            anywhere,
            anywhere,
        ],
        out_specs=[pair_spec, anywhere, anywhere, anywhere] + [whole(s) for s in grad_shapes],
        scratch_shapes=[dma((3,))],
        compiler_params=pltpu.CompilerParams(
            dimension_semantics=("arbitrary",), vmem_limit_bytes=40 * 1024 * 1024
        ),
        name="pair_grad",
    )(
        atom_pair,
        dl,
        t,
        mean,
        wide,
        red1,
        red2,
        named["pair_gain"].reshape(1, -1),
        named["pair_weight"],
        layer,
        agrad,
        cgrad,
    )
    pgrad, layer, agrad, cgrad, *weight_grads = finals
    weight_grads = [g.reshape(named[n].shape) for g, n in zip(weight_grads, GRADS)]
    return (layer, agrad, pgrad, cgrad, *weight_grads)


def solution(mesh):
    atoms = P("dp", "atoms", None)
    pair = P("dp", None, "atoms", None)
    return jax.shard_map(
        functools.partial(shards, mesh.shape["atoms"], mesh.shape["dp"]),
        mesh=mesh,
        in_specs=(atoms, atoms, pair, P("dp"), atoms) + (P(),) * len(GRADS),
        out_specs=(atoms, atoms, pair, atoms) + (P(),) * len(GRADS),
        check_vma=False,
    )
```

time: 385 us -> 65.1 us (0.17); the launches traced: 379 us -> 64.6 us
  waiting for transfers between devices: 130 us -> 0 us
  matrix products: 80.7 us -> 0 us
  local copies, waits for them, and re-layouts: 79.7 us -> 12.6 us
  other arithmetic: 61.7 us -> 0 us
  Pallas kernels: 0 us -> 51.3 us
  between operations: 15.7 us -> 0.71 us
  starting transfers between devices: 11.1 us -> 0 us
    psum x1 -> x0, waiting for transfers between devices: 130 us -> none  [shards(): flattened = lax.psum(flattened, ('dp', 'atoms'))]
    dot_general x42 -> x0, matrix products: 80.7 us -> none  [the longest x1 21.5 us: shards(): jnp.einsum('ihak,ch->icak', term_grad, pair_weight, precision=highest)]
    pallas_call x0 -> x2, Pallas kernels: none -> 51.3 us  [the longest x1 44.8 us: shards(): pl.pallas_call(functools.partial(main_kernel, n_a, n_d), out_shape=[sds(b...]
    concatenate x3 -> x0, local copies, waits for them, and re-layouts: 27.1 us -> none  [the longest x1 26.3 us: shards(): flattened = jnp.concatenate([member.reshape(-1) for member in weight_grads])]
    sub x2 -> x0, other arithmetic: 23.2 us -> none  [the longest x1 23.2 us: shards(): logits_grad = jnp.where(mask_full, probs * (probs_grad - row_inner), 0.0)]
    reshape x12 -> x0, local copies, waits for them, and re-layouts: 19 us -> none  [the longest x5 5.44 us: split_flat(): summed.append(flattened[offset:offset + extent].reshape(member.shape))]
    reduce_sum x9 -> x0, other arithmetic: 18.3 us -> none  [the longest x3 8.07 us: normalize(): centre = values - jnp.mean(values, axis=axis, keepdims=True)]
    ppermute x4 -> x0, starting transfers between devices: 11.1 us -> none  [the longest x2 8.12 us: with_halo(): before = lax.ppermute(last, axis, up)]
  transfers between devices with their start and end apart: 5 -> 0, of which waited for: 1 -> 0; matrix products, arithmetic and copies ran while one was open for 22% -> 0% of each run, Pallas kernels for 0% -> 0%
where the time goes in v1:
time: 65.1 us; the launch traced here: 64.6 us
  Pallas kernels  51.3 us (79%)
  local copies, waits for them, and re-layouts  12.6 us (19%)
  between operations  0.71 us (1%)
    pallas_call x1, Pallas kernels, shards(): pl.pallas_call(functools.partial(main_kernel, n_a, n_d), out_shape=[sds(b...  44.8 us
    unnamed x26, local copies, waits for them, and re-layouts  12.6 us
    pallas_call x1, Pallas kernels, shards(): pl.pallas_call(functools.partial(pair_kernel, steps), grid=(steps,), out_...  6.52 us

profile of v1, /device:TPU:0, one launch (start us, length us, event | category | flops | bytes accessed | tf_op | source)
XLA Modules:
  0.0 64.6 jit_solution(6182509271710561230)
XLA Ops:
  0.7 1.4 %copy.55.pair_weight = f32[16,4]{1,0:T(8,128)} copy(f32[16,4]{0,1:T(4,128)} %param.43) | data formatting | bytes 512 | tf_op args[15]
  2.0 0.0 copy-start
  2.0 44.8 %block.1 = (bf16[4,256,128]{2,1,0:T(8,128)(2,1)}, f32[4,256,128]{2,1,0:T(8,128)}, f32[4,256,128]{2,1,0:T(8,128)}, bf16[4,8,128,128]{3,2,1,0:T(8,128)(2,1)}, f32[...) custom-call(s32[4]{0:T(128)} %counts.1, ...), custom_call_target="tpu_custom_call" | custom-call | tf_op jit(solution)/shard_map/block/pallas_call | solution.py:911
  46.8 0.0 copy-done
  46.8 0.0 copy-start.1
  46.8 1.2 %copy-done.1 = bf16[4,8,128,128]{3,2,1,0:T(8,128)(2,1)S(1)} copy-done((bf16[4,8,128,128]{3,2,1,0:T(8,128)(2,1)S(1)}, bf16[4,8,128,128]{3,2,1,0:T(8,128)(2,1)}, u32[]{:S(2)}) %copy-start.1) | copy-done | bytes 1048600
  48.0 0.0 copy-start.2
  48.0 1.0 %copy-done.2 = f32[4,256,128]{2,1,0:T(8,128)S(1)} copy-done((f32[4,256,128]{2,1,0:T(8,128)S(1)}, f32[4,256,128]{2,1,0:T(8,128)}, u32[]{:S(2)}) %copy-start.2) | copy-done | bytes 524312
  49.1 0.0 copy-start.3
  49.1 1.0 %copy-done.3 = f32[4,256,128]{2,1,0:T(8,128)S(1)} copy-done((f32[4,256,128]{2,1,0:T(8,128)S(1)}, f32[4,256,128]{2,1,0:T(8,128)}, u32[]{:S(2)}) %copy-start.3) | copy-done | bytes 524312
  50.1 0.0 copy-start.4
  50.1 1.0 %copy-done.4 = f32[4,256,128]{2,1,0:T(8,128)S(1)} copy-done((f32[4,256,128]{2,1,0:T(8,128)S(1)}, f32[4,256,128]{2,1,0:T(8,128)}, u32[]{:S(2)}) %copy-start.4) | copy-done | bytes 524312
  51.2 0.0 copy-start.5
  51.2 1.0 %copy-done.5 = f32[4,256,128]{2,1,0:T(8,128)S(1)} copy-done((f32[4,256,128]{2,1,0:T(8,128)S(1)}, f32[4,256,128]{2,1,0:T(8,128)}, u32[]{:S(2)}) %copy-start.5) | copy-done | bytes 524312
  52.2 0.0 copy-start.6
  52.2 1.0 %copy-done.6 = bf16[8,192,128]{2,1,0:T(8,128)(2,1)S(1)} copy-done((bf16[8,192,128]{2,1,0:T(8,128)(2,1)S(1)}, bf16[8,192,128]{2,1,0:T(8,128)(2,1)}, u32[]{:S(2)}) %copy-start.6) | copy-done | bytes 393240
  53.2 0.0 copy-start.7
  53.2 0.9 %copy-done.7 = bf16[4,256,128]{2,1,0:T(8,128)(2,1)S(1)} copy-done((bf16[4,256,128]{2,1,0:T(8,128)(2,1)S(1)}, bf16[4,256,128]{2,1,0:T(8,128)(2,1)}, u32[]{:S(2)}) %copy-start.7) | copy-done | bytes 262168
  54.1 0.9 %copy-done.8 = bf16[512,256]{1,0:T(8,128)(2,1)S(1)} copy-done((bf16[512,256]{1,0:T(8,128)(2,1)S(1)}, bf16[512,256]{1,0:T(8,128)(2,1)}, u32[]{:S(2)}) %copy-start.8) | copy-done | bytes 262168
  55.1 0.9 %copy-done.9 = bf16[8,96,128]{2,1,0:T(8,128)(2,1)S(1)} copy-done((bf16[8,96,128]{2,1,0:T(8,128)(2,1)S(1)}, bf16[8,96,128]{2,1,0:T(8,128)(2,1)}, u32[]{:S(2)}) %copy-start.9) | copy-done | bytes 196632
  56.0 0.7 %copy-done.10 = f32[16,4]{1,0:T(8,128)S(1)} copy-done((f32[16,4]{1,0:T(8,128)S(1)}, f32[16,4]{1,0:T(8,128)}, u32[]{:S(2)}) %copy-start.10) | copy-done | bytes 280
  56.7 0.7 %copy-done.11 = f32[16]{0:T(128)S(1)} copy-done((f32[16]{0:T(128)S(1)}, f32[16]{0:T(128)}, u32[]{:S(2)}) %copy-start.11) | copy-done | bytes 88
  57.4 6.5 %pair_grad.1 = (f32[4,16,256,128]{3,2,1,0:T(8,128)}, bf16[4,256,128]{2,1,0:T(8,128)(2,1)}, f32[4,256,128]{2,1,0:T(8,128)}, f32[4,256,128]{2,1,0:T(8,128)}, f32[1...) custom-call(bf16[4,16,256,128]{3,2,1,0:T(8,128)(2,1)S(1)} %copy-done, ...), custom_call_target="tpu_custom_call" | custom-call | tf_op jit(solution)/shard_map/pair_grad/pallas_call | solution.py:1012
  63.9 0.7 %copy.57 = f32[16,4]{0,1:T(4,128)} copy(f32[16,4]{1,0:T(8,128)S(1)} %get-tuple-element.113) | data formatting | bytes 512
  (4 shorter events, 0.0 us)
Async XLA Ops:
  2.0 44.8 %copy-start = (bf16[4,16,256,128]{3,2,1,0:T(8,128)(2,1)S(1)}, bf16[4,16,256,128]{3,2,1,0:T(8,128)(2,1)}, u32[]{:S(2)}) copy-start(bf16[4,16,256,128]{3,2,1,0:T(8,128)(2,1)} %pair.1) | copy-start | bytes 12582916
  46.8 1.2 %copy-start.1 = (bf16[4,8,128,128]{3,2,1,0:T(8,128)(2,1)S(1)}, bf16[4,8,128,128]{3,2,1,0:T(8,128)(2,1)}, u32[]{:S(2)}) copy-start(bf16[4,8,128,128]{3,2,1,0:T(8,128)(2,1)} %get-tuple-element.63.dl) | copy-start | bytes 3145732
  48.0 1.0 %copy-start.2 = (f32[4,256,128]{2,1,0:T(8,128)S(1)}, f32[4,256,128]{2,1,0:T(8,128)}, u32[]{:S(2)}) copy-start(f32[4,256,128]{2,1,0:T(8,128)} %get-tuple-element.70.agrad_in) | copy-start | bytes 1572868
  49.1 1.0 %copy-start.3 = (f32[4,256,128]{2,1,0:T(8,128)S(1)}, f32[4,256,128]{2,1,0:T(8,128)}, u32[]{:S(2)}) copy-start(f32[4,256,128]{2,1,0:T(8,128)} %get-tuple-element.71.cgrad_in) | copy-start | bytes 1572868
  50.1 1.0 %copy-start.4 = (f32[4,256,128]{2,1,0:T(8,128)S(1)}, f32[4,256,128]{2,1,0:T(8,128)}, u32[]{:S(2)}) copy-start(f32[4,256,128]{2,1,0:T(8,128)} %get-tuple-element.64.t) | copy-start | bytes 1572868
  51.2 1.0 %copy-start.5 = (f32[4,256,128]{2,1,0:T(8,128)S(1)}, f32[4,256,128]{2,1,0:T(8,128)}, u32[]{:S(2)}) copy-start(f32[4,256,128]{2,1,0:T(8,128)} %get-tuple-element.65.mean) | copy-start | bytes 1572868
  52.2 1.0 %copy-start.6 = (bf16[8,192,128]{2,1,0:T(8,128)(2,1)S(1)}, bf16[8,192,128]{2,1,0:T(8,128)(2,1)}, u32[]{:S(2)}) copy-start(bf16[8,192,128]{2,1,0:T(8,128)(2,1)} %get-tuple-element.67) | copy-start | bytes 1179652
  53.2 0.9 %copy-start.7 = (bf16[4,256,128]{2,1,0:T(8,128)(2,1)S(1)}, bf16[4,256,128]{2,1,0:T(8,128)(2,1)}, u32[]{:S(2)}) copy-start(bf16[4,256,128]{2,1,0:T(8,128)(2,1)} %get-tuple-element.69.layer_in) | copy-start | bytes 786436
  54.1 0.9 %copy-start.8 = (bf16[512,256]{1,0:T(8,128)(2,1)S(1)}, bf16[512,256]{1,0:T(8,128)(2,1)}, u32[]{:S(2)}) copy-start(bf16[512,256]{1,0:T(8,128)(2,1)} %get-tuple-element.66.wide) | copy-start | bytes 786436
  55.1 0.9 %copy-start.9 = (bf16[8,96,128]{2,1,0:T(8,128)(2,1)S(1)}, bf16[8,96,128]{2,1,0:T(8,128)(2,1)}, u32[]{:S(2)}) copy-start(bf16[8,96,128]{2,1,0:T(8,128)(2,1)} %get-tuple-element.68) | copy-start | bytes 589828
  56.0 0.7 %copy-start.10 = (f32[16,4]{1,0:T(8,128)S(1)}, f32[16,4]{1,0:T(8,128)}, u32[]{:S(2)}) copy-start(f32[16,4]{1,0:T(8,128)} %copy.55.pair_weight) | copy-start | bytes 772
  56.7 0.7 %copy-start.11 = (f32[16]{0:T(128)S(1)}, f32[16]{0:T(128)}, u32[]{:S(2)}) copy-start(f32[16]{0:T(128)} %param.42) | copy-start | bytes 196

commit v2 on v1

v2 whole, which is shorter than its diff:
```python
import functools

import jax
import jax.numpy as jnp
from jax import lax
from jax.experimental import pallas as pl
from jax.experimental.pallas import tpu as pltpu
from jax.sharding import PartitionSpec as P

QW = 32
KW = 128
HALO = 48
SPREAD = KW // QW
EPSILON = 1e-05
MASKED = -1000000000.0
HIGHEST = lax.Precision.HIGHEST
MESH = pl.DeviceIdType.MESH
PROJECT_ITEMS = 2
PAIR_ITEMS = 1
ATTEND_ITEMS = 2
MIDDLE_ITEMS = 2
BACK_ITEMS = 1
FINISH_ITEMS = 2
F32 = jnp.float32
BF16 = jnp.bfloat16

GROUP_ONE = (
    "hidden_gate_a",
    "hidden_gate_b",
    "hidden_up_a",
    "hidden_up_b",
    "hidden_down_a",
    "hidden_down_b",
    "output_weight",
    "branch_gate",
    "closing_gate",
    "second_scale",
    "second_shift",
    "gate_weight",
)
GROUP_TWO = ("query_weight", "key_weight", "value_weight", "first_scale", "first_shift")
VECTORS = (
    "first_gain",
    "first_lift",
    "query_bias",
    "branch_lift",
    "second_gain",
    "second_lift",
    "closing_lift",
)


def mm(a, b, precision=None):
    return lax.dot_general(
        a, b, (((1,), (0,)), ((), ())), precision=precision, preferred_element_type=F32
    )


def mm_t(a, b, precision=None):
    return lax.dot_general(
        a, b, (((1,), (1,)), ((), ())), precision=precision, preferred_element_type=F32
    )


def t_mm(a, b):
    return lax.dot_general(a, b, (((0,), (0,)), ((), ())), preferred_element_type=F32)


def sigmoid(v):
    return 0.5 * jnp.tanh(0.5 * v) + 0.5


def lane_mean(v):
    return jnp.mean(v, axis=-1, keepdims=True)


def normalize(v):
    centre = v - lane_mean(v)
    inverse = lax.rsqrt(lane_mean(centre * centre) + EPSILON)
    return centre * inverse, jnp.broadcast_to(inverse, v.shape)


def normalize_back(normed, inverse, grads):
    return inverse * (grads - lane_mean(grads) - normed * lane_mean(grads * normed))


def lanes(*parts):
    return jnp.concatenate(parts, axis=1)


def rows(*parts):
    return jnp.concatenate(parts, axis=0)


def col_sum(v):
    return jnp.sum(v, axis=0, keepdims=True)


def iota(shape, axis):
    return lax.broadcasted_iota(jnp.int32, shape, axis)


def shard_rows(total, peers):
    return -(-total // (16 * peers)) * 16


def main_kernel(
    n_a,
    n_d,
    counts,
    single,
    cond,
    cot,
    pair_hbm,
    first_gain,
    first_scale,
    first_lift,
    first_shift,
    query_weight,
    query_bias,
    key_weight,
    value_weight,
    gate_weight,
    pair_gain,
    pair_weight,
    output_weight,
    branch_gate,
    branch_lift,
    second_gain,
    second_scale,
    second_lift,
    second_shift,
    hidden_gate,
    hidden_up,
    hidden_down,
    closing_gate,
    closing_lift,
    layer_o,
    agrad_o,
    cgrad_o,
    pgrad_o,
    red1_s,
    red2_s,
    pair_s,
    kv_s,
    q_s,
    first_s,
    chat_s,
    cinv_s,
    shat_s,
    sinv_s,
    sig_s,
    gating_s,
    term_s,
    probs_s,
    inv_s,
    mean_s,
    att_s,
    mid_grad_s,
    cnorm_s,
    cdir_s,
    dlow_s,
    glow_s,
    dl_s,
    t_s,
    dq_s,
    kvg_s,
    wide_s,
    widet_s,
    headmask_s,
    pacc_s,
    acc1_s,
    acc2_s,
    halo_send,
    halo_recv,
    send1,
    recv1,
    zall1,
    send2,
    recv2,
    zall2,
    pair_sem,
    kv_send_sem,
    kv_recv_sem,
    hg_send_sem,
    hg_recv_sem,
    rs1_send,
    rs1_recv,
    z1_send,
    z1_recv,
    ag1_send,
    ag1_recv,
    rs2_send,
    rs2_recv,
    z2_send,
    z2_recv,
    ag2_send,
    ag2_recv,
):
    items, length, width = single.shape
    windows = length // QW
    heads, channels = pair_weight.shape
    head_dim = width // heads
    factor = head_dim ** (-0.5)
    me = lax.axis_index("atoms")
    me_d = lax.axis_index("dp")
    anchor = me * length
    has_left = me > 0
    has_right = me < n_a - 1

    def pair_copy(i):
        return pltpu.make_async_copy(pair_hbm.at[i], pair_s.at[i], pair_sem.at[i])

    for i in range(items):
        pair_copy(i).start()

    kv_s[:, 0:HALO, :] = jnp.zeros((items, HALO, 2 * width), BF16)
    kv_s[:, HALO + length : 2 * HALO + length, :] = jnp.zeros((items, HALO, 2 * width), BF16)
    halo_recv[...] = jnp.zeros(halo_recv.shape, BF16)

    barrier = pltpu.get_barrier_semaphore()

    def greet_atoms(k, carry):
        pl.semaphore_signal(
            barrier, inc=1, device_id={"atoms": lax.rem(me + k, n_a)}, device_id_type=MESH
        )
        return carry

    def greet_dp(k, carry):
        pl.semaphore_signal(
            barrier, inc=1, device_id={"dp": lax.rem(me_d + k, n_d)}, device_id_type=MESH
        )
        return carry

    lax.fori_loop(1, n_a, greet_atoms, 0)
    lax.fori_loop(1, n_d, greet_dp, 0)

    hq = heads * QW
    cq = channels * QW
    headmask_s[...] = jnp.where(
        iota((hq, width), 0) // QW == iota((hq, width), 1) // head_dim, 1.0, 0.0
    ).astype(BF16)
    pick_head = jnp.where(iota((hq, heads), 0) // QW == iota((hq, heads), 1), 1.0, 0.0)
    weighted = mm(pick_head, pair_weight[...], HIGHEST) * pair_gain[...]
    weighted = weighted - lane_mean(weighted)
    spread = jnp.where(iota((channels, cq), 0) == iota((channels, cq), 1) // QW, 1.0, 0.0).astype(
        BF16
    )
    same_row = iota((hq, cq), 0) % QW == iota((hq, cq), 1) % QW
    high = weighted.astype(BF16)
    low = (weighted - high.astype(F32)).astype(BF16)
    wide_high = jnp.where(same_row, mm(high, spread), 0.0)
    wide_low = jnp.where(same_row, mm(low, spread), 0.0)
    wide_s[0:hq, :] = wide_high.astype(BF16)
    wide_s[hq : 2 * hq, :] = wide_low.astype(BF16)
    widet_s[:, 0:hq] = wide_high.T.astype(BF16)
    widet_s[:, hq : 2 * hq] = wide_low.T.astype(BF16)

    acc1_s[...] = jnp.zeros(acc1_s.shape, F32)
    acc2_s[...] = jnp.zeros(acc2_s.shape, F32)
    pacc_s[...] = jnp.zeros(pacc_s.shape, F32)

    def add1(name, value):
        at = GROUP_ONE.index(name) * width
        acc1_s[at : at + value.shape[0], :] += value

    def add2(name, value):
        at = GROUP_TWO.index(name) * width
        acc2_s[at : at + value.shape[0], :] += value

    vector_at = len(GROUP_TWO) * width

    def add_vector(name, value):
        at = vector_at + VECTORS.index(name)
        acc2_s[at : at + 1, :] += value

    pair_at = vector_at + 8

    def steps(count, body):
        def step(s, carry):
            body(s * count)
            return carry

        lax.fori_loop(0, items // count, step, 0)

    def of_items(ref, i, count):
        return ref[pl.ds(i, count)].reshape(count * length, ref.shape[-1])

    def rows_of(i, count):
        return pl.ds(pl.multiple_of(i * length, length), count * length)

    def alive(i, count):
        place = anchor + iota((length, width), 0)
        return rows(*[jnp.where(place < counts[i + k], 1.0, 0.0) for k in range(count)])

    def project(i):
        n = PROJECT_ITEMS
        at = rows_of(i, n)
        single_hat, single_inv = normalize(of_items(single, i, n).astype(F32))
        cond_hat, cond_inv = normalize(of_items(cond, i, n).astype(F32))
        low1 = (cond_hat * first_gain[...]).astype(BF16)
        pre = mm(low1, lanes(first_scale[...], first_shift[...]))
        scaling = sigmoid(pre[:, :width] + first_lift[...])
        first = (scaling * single_hat + pre[:, width:]).astype(BF16)
        qkvg = mm(
            first, lanes(query_weight[...], key_weight[...], value_weight[...], gate_weight[...])
        )
        q_s[at, :] = (qkvg[:, :width] + query_bias[...]).astype(BF16)
        for k in range(n):
            kv_s[i + k, HALO : HALO + length, :] = qkvg[
                k * length : (k + 1) * length, width : 3 * width
            ].astype(BF16)
        gating_s[at, :] = sigmoid(qkvg[:, 3 * width :])
        first_s[at, :] = first
        shat_s[at, :] = single_hat
        sinv_s[at, :] = single_inv
        chat_s[at, :] = cond_hat
        cinv_s[at, :] = cond_inv
        sig_s[at, :] = scaling

    steps(PROJECT_ITEMS, project)

    pl.semaphore_wait(barrier, n_a - 1 + n_d - 1)

    def kv_right():
        return pltpu.make_async_remote_copy(
            src_ref=kv_s.at[:, pl.ds(length, HALO), :],
            dst_ref=kv_s.at[:, pl.ds(0, HALO), :],
            send_sem=kv_send_sem.at[0],
            recv_sem=kv_recv_sem.at[0],
            device_id={"atoms": lax.rem(me + 1, n_a)},
            device_id_type=MESH,
        )

    def kv_left():
        return pltpu.make_async_remote_copy(
            src_ref=kv_s.at[:, pl.ds(HALO, HALO), :],
            dst_ref=kv_s.at[:, pl.ds(HALO + length, HALO), :],
            send_sem=kv_send_sem.at[1],
            recv_sem=kv_recv_sem.at[1],
            device_id={"atoms": lax.rem(me + n_a - 1, n_a)},
            device_id_type=MESH,
        )

    @pl.when(has_right)
    def _():
        kv_right().start()

    @pl.when(has_left)
    def _():
        kv_left().start()

    def window_at(i, w):
        return pl.ds(pl.multiple_of(i * length + w * QW, QW), QW)

    def pair_rows(i, w):
        return pair_s[i, :, w * QW : (w + 1) * QW, :]

    def pair_forward(i):
        for k in range(PAIR_ITEMS):
            pair_copy(i + k).wait()
        wide = wide_s[...]
        for k in range(PAIR_ITEMS):
            for w in range(0, windows, 2):
                invs = []
                for v in (w, w + 1):
                    block = pair_rows(i + k, v).astype(F32)
                    mean = jnp.mean(block, axis=0)
                    centre = block - mean[None]
                    inv = lax.rsqrt(jnp.mean(centre * centre, axis=0) + EPSILON)
                    mean_s[window_at(i + k, v), :] = mean
                    inv_s[window_at(i + k, v), :] = inv
                    invs.append(inv)
                both = lanes(
                    pair_rows(i + k, w).reshape(cq, KW), pair_rows(i + k, w + 1).reshape(cq, KW)
                )
                product = mm(wide, both)
                product = product[:hq] + product[hq:]
                for v in (0, 1):
                    part = product[:, v * KW : (v + 1) * KW].reshape(heads, QW, KW)
                    term_s[i + k, w + v] = (part * invs[v][None]).reshape(hq, KW)

    steps(PAIR_ITEMS, pair_forward)

    @pl.when(has_right)
    def _():
        kv_right().wait_send()

    @pl.when(has_left)
    def _():
        kv_left().wait_send()

    @pl.when(has_left)
    def _():
        kv_right().wait_recv()

    @pl.when(has_right)
    def _():
        kv_left().wait_recv()

    def spread_heads(block):
        return rows(*([block] * heads)) * headmask_s[...]

    def gather_heads(wide_block):
        lane = iota((QW, width), 1)
        result = wide_block[(heads - 1) * QW :]
        for h in range(heads - 2, -1, -1):
            result = jnp.where(
                lane < (h + 1) * head_dim, wide_block[h * QW : (h + 1) * QW], result
            )
        return result

    def keys_of(i, w):
        return kv_s[i, w * QW : w * QW + KW, 0:width]

    def values_of(i, w):
        return kv_s[i, w * QW : w * QW + KW, width : 2 * width]

    def windows_of(i, count):
        return [(i + k, w) for k in range(count) for w in range(windows)]

    def attend(i):
        here = windows_of(i, ATTEND_ITEMS)
        scores = [mm_t(spread_heads(q_s[window_at(*a), :]), keys_of(*a)) for a in here]
        logits = []
        for a, score in zip(here, scores):
            place = anchor + (a[1] * QW - HALO) + iota((1, KW), 1)
            valid = (place >= 0) & (place < counts[a[0]])
            logits.append(jnp.where(valid, score * factor + term_s[a], MASKED))
        tops = [jnp.max(v, axis=-1, keepdims=True) for v in logits]
        raised = [jnp.exp(v - top) for v, top in zip(logits, tops)]
        totals = [jnp.sum(v, axis=-1, keepdims=True) for v in raised]
        for a, up, total in zip(here, raised, totals):
            probs = up * (1.0 / total)
            probs_s[a] = probs
            att_s[window_at(*a), :] = gather_heads(mm(probs.astype(BF16), values_of(*a)))

    steps(ATTEND_ITEMS, attend)

    def middle(i):
        n = MIDDLE_ITEMS
        at = rows_of(i, n)
        live = alive(i, n)
        att = att_s[at, :]
        gating = gating_s[at, :]
        cond_hat = chat_s[at, :]
        cond_rows = of_items(cond, i, n)
        gated = (gating * att).astype(BF16)
        branch = mm(gated, output_weight[...])
        zeros = mm(cond_rows, lanes(branch_gate[...], closing_gate[...]))
        zero_one = sigmoid(zeros[:, :width] + branch_lift[...])
        zero_two = sigmoid(zeros[:, width:] + closing_lift[...])
        live_one = live * zero_one
        live_two = live * zero_two
        mid = of_items(single, i, n).astype(F32) + live_one * branch
        mid_hat, mid_inv = normalize(mid)
        low2 = (cond_hat * second_gain[...]).astype(BF16)
        scale_shift = lanes(second_scale[...], second_shift[...])
        pre = mm(low2, scale_shift)
        scaling = sigmoid(pre[:, :width] + second_lift[...])
        second = (scaling * mid_hat + pre[:, width:]).astype(BF16)
        gate_up = lanes(hidden_gate[...], hidden_up[...])
        pre2 = mm(second, gate_up)
        inner = hidden_gate.shape[1]
        gate_pre, up_pre = pre2[:, :inner], pre2[:, inner:]
        gate_sig = sigmoid(gate_pre)
        gate_silu = gate_pre * gate_sig
        hidden = (gate_silu * up_pre).astype(BF16)
        closing = mm(hidden, hidden_down[...])
        layer_o[pl.ds(i, n)] = (
            (mid + live_two * closing).astype(BF16).reshape(n, length, width)
        )
        out_grad = of_items(cot, i, n).astype(F32)
        closing_full = out_grad * live_two
        closing_grad = closing_full.astype(BF16)
        zero_two_pre = closing_full * closing * (1.0 - zero_two)
        zero_two_low = zero_two_pre.astype(BF16)
        add1("hidden_down_a", t_mm(hidden, closing_grad))
        add_vector("closing_lift", col_sum(zero_two_pre))
        hidden_grad = mm_t(closing_grad, hidden_down[...])
        gate_pre_grad = (hidden_grad * up_pre * (gate_sig + gate_silu * (1.0 - gate_sig))).astype(
            BF16
        )
        up_pre_grad = (hidden_grad * gate_silu).astype(BF16)
        gate_up_grad = lanes(gate_pre_grad, up_pre_grad)
        wide_grad = t_mm(second, gate_up_grad)
        for k, name in enumerate(GROUP_ONE[:4]):
            add1(name, wide_grad[:, k * width : (k + 1) * width])
        second_grad = mm_t(gate_up_grad, gate_up)
        scaled_grad = second_grad * scaling
        before = scaled_grad * mid_hat * (1.0 - scaling)
        both = lanes(before.astype(BF16), second_grad.astype(BF16))
        both_grad = t_mm(low2, both)
        add1("second_scale", both_grad[:, :width])
        add1("second_shift", both_grad[:, width:])
        add_vector("second_lift", col_sum(before))
        cond_normed = mm_t(both, scale_shift)
        add_vector("second_gain", col_sum(cond_normed * cond_hat))
        cnorm_s[at, :] = cond_normed * second_gain[...]
        mid_grad = out_grad + normalize_back(mid_hat, mid_inv, scaled_grad)
        mid_grad_s[at, :] = mid_grad
        branch_full = mid_grad * live_one
        branch_grad = branch_full.astype(BF16)
        zero_one_pre = branch_full * branch * (1.0 - zero_one)
        add_vector("branch_lift", col_sum(zero_one_pre))
        zero_grads = lanes(zero_one_pre.astype(BF16), zero_two_low)
        gate_grads = t_mm(cond_rows, zero_grads)
        add1("branch_gate", gate_grads[:, :width])
        add1("closing_gate", gate_grads[:, width:])
        cdir_s[at, :] = mm_t(zero_grads, lanes(branch_gate[...], closing_gate[...]))
        add1("output_weight", t_mm(gated, branch_grad))
        attended_grad = mm_t(branch_grad, output_weight[...]) * gating
        dlow_s[at, :] = attended_grad.astype(BF16)
        gate_low = (attended_grad * att * (1.0 - gating)).astype(BF16)
        glow_s[at, :] = gate_low
        add1("gate_weight", t_mm(first_s[at, :], gate_low))

    steps(MIDDLE_ITEMS, middle)

    class Sum:
        def __init__(self, acc, send, recv, zall, red, sems):
            self.acc, self.send, self.recv, self.zall, self.red = acc, send, recv, zall, red
            self.rs_send, self.rs_recv, self.z_send, self.z_recv, self.ag_send, self.ag_recv = sems
            self.shard = send.shape[1]

        def scatter_copy(self, to, at):
            return pltpu.make_async_remote_copy(
                src_ref=self.send.at[to],
                dst_ref=self.recv.at[at],
                send_sem=self.rs_send.at[to],
                recv_sem=self.rs_recv.at[at],
                device_id={"atoms": to},
                device_id_type=MESH,
            )

        def dp_copy(self, to, at):
            return pltpu.make_async_remote_copy(
                src_ref=self.zall.at[me_d],
                dst_ref=self.zall.at[at],
                send_sem=self.z_send.at[to],
                recv_sem=self.z_recv.at[at],
                device_id={"dp": to},
                device_id_type=MESH,
            )

        def gather_copy(self, to, at):
            return pltpu.make_async_remote_copy(
                src_ref=self.red.at[me],
                dst_ref=self.red.at[at],
                send_sem=self.ag_send.at[to],
                recv_sem=self.ag_recv.at[at],
                device_id={"atoms": to},
                device_id_type=MESH,
            )

        def scatter(self):
            self.send[...] = self.acc[...].astype(BF16).reshape(self.send.shape)

            def go(k, carry):
                self.scatter_copy(lax.rem(me + k, n_a), me).start()
                return carry

            lax.fori_loop(1, n_a, go, 0)

        def over_dp(self):
            start = pl.multiple_of(me * self.shard, 16)
            total = self.acc[pl.ds(start, self.shard), :]
            for k in range(1, n_a):
                peer = lax.rem(me + k, n_a)
                self.scatter_copy(peer, peer).wait_recv()
                total = total + self.recv[peer].astype(F32)
            self.zall[me_d] = total.astype(BF16)

            def go(k, carry):
                self.dp_copy(lax.rem(me_d + k, n_d), me_d).start()
                return carry

            lax.fori_loop(1, n_d, go, 0)

        def gather(self):
            def come(k, carry):
                peer = lax.rem(me_d + k, n_d)
                self.dp_copy(peer, peer).wait_recv()
                return carry

            lax.fori_loop(1, n_d, come, 0)
            total = self.zall[0].astype(F32)
            for d in range(1, n_d):
                total = total + self.zall[d].astype(F32)
            self.red[me] = total.astype(BF16)

            def go(k, carry):
                self.gather_copy(lax.rem(me + k, n_a), me).start()
                return carry

            lax.fori_loop(1, n_a, go, 0)

        def finish(self):
            def end(k, carry):
                peer = lax.rem(me + k, n_a)
                self.gather_copy(peer, peer).wait_recv()
                self.gather_copy(peer, peer).wait_send()
                self.scatter_copy(peer, peer).wait_send()
                return carry

            lax.fori_loop(1, n_a, end, 0)

            def end_dp(k, carry):
                peer = lax.rem(me_d + k, n_d)
                self.dp_copy(peer, peer).wait_send()
                return carry

            lax.fori_loop(1, n_d, end_dp, 0)

    sum1 = Sum(
        acc1_s,
        send1,
        recv1,
        zall1,
        red1_s,
        (rs1_send, rs1_recv, z1_send, z1_recv, ag1_send, ag1_recv),
    )
    sum2 = Sum(
        acc2_s,
        send2,
        recv2,
        zall2,
        red2_s,
        (rs2_send, rs2_recv, z2_send, z2_recv, ag2_send, ag2_recv),
    )
    sum1.scatter()

    def halo_right(i):
        return pltpu.make_async_remote_copy(
            src_ref=halo_send.at[i, 1],
            dst_ref=halo_recv.at[i, 0],
            send_sem=hg_send_sem.at[i, 1],
            recv_sem=hg_recv_sem.at[i, 0],
            device_id={"atoms": lax.rem(me + 1, n_a)},
            device_id_type=MESH,
        )

    def halo_left(i):
        return pltpu.make_async_remote_copy(
            src_ref=halo_send.at[i, 0],
            dst_ref=halo_recv.at[i, 1],
            send_sem=hg_send_sem.at[i, 0],
            recv_sem=hg_recv_sem.at[i, 1],
            device_id={"atoms": lax.rem(me + n_a - 1, n_a)},
            device_id_type=MESH,
        )

    def attend_back(i):
        here = windows_of(i, BACK_ITEMS)
        wide_grads = [spread_heads(dlow_s[window_at(*a), :]) for a in here]
        probs_grads = [mm_t(wide, values_of(*a)) for a, wide in zip(here, wide_grads)]
        inners = [
            jnp.sum(grad * probs_s[a], axis=-1, keepdims=True)
            for a, grad in zip(here, probs_grads)
        ]
        value_parts = [t_mm(probs_s[a].astype(BF16), wide) for a, wide in zip(here, wide_grads)]
        key_parts = []
        for a, grad, inner in zip(here, probs_grads, inners):
            at = window_at(*a)
            logits_grad = probs_s[a] * (grad - inner)
            low = logits_grad.astype(BF16)
            dq_s[at, :] = gather_heads(mm(low, keys_of(*a))) * factor
            key_parts.append(t_mm(low, spread_heads(q_s[at, :])) * factor)
            inv = inv_s[at, :]
            by_head = logits_grad.reshape(heads, QW, KW)
            dl_s[a] = (by_head * inv[None]).astype(BF16).reshape(hq, KW)
            dot = jnp.sum(by_head * term_s[a].reshape(heads, QW, KW), axis=0)
            t_s[at, :] = dot * inv * inv * (1.0 / channels)
        for k in range(BACK_ITEMS):
            for parts, at in ((key_parts, 0), (value_parts, width)):
                part = parts[k * windows : (k + 1) * windows]
                for b in range(windows + SPREAD - 1):
                    block = None
                    for w in range(max(0, b - SPREAD + 1), min(windows - 1, b) + 1):
                        piece = part[w][(b - w) * QW : (b - w + 1) * QW]
                        block = piece if block is None else block + piece
                    kvg_s[i + k, b * QW : (b + 1) * QW, at : at + width] = block
            halo_send[i + k, 0] = kvg_s[i + k, 0:HALO, :].astype(BF16)
            halo_send[i + k, 1] = kvg_s[i + k, HALO + length : 2 * HALO + length, :].astype(BF16)

            @pl.when(has_right)
            def _(k=k):
                halo_right(i + k).start()

            @pl.when(has_left)
            def _(k=k):
                halo_left(i + k).start()

        pair_all = lanes(*[pair_rows(*a).reshape(cq, KW) for a in here])
        grads_all = lanes(*[dl_s[a] for a in here])
        pacc_s[...] += mm_t(pair_all, grads_all)

    steps(BACK_ITEMS, attend_back)

    diagonal = jnp.where(iota((cq, hq), 0) % QW == iota((cq, hq), 1) % QW, pacc_s[...], 0.0)
    by_channel = jnp.sum(diagonal.reshape(channels, QW, hq), axis=1)
    fold = jnp.where(iota((hq, width), 0) // QW == iota((hq, width), 1), 1.0, 0.0)
    pair_sums = mm(by_channel, fold, HIGHEST)
    acc2_s[pair_at : pair_at + channels, :] = pair_sums - jnp.mean(
        pair_sums, axis=0, keepdims=True
    )

    def finish_rows(i):
        n = FINISH_ITEMS
        at = rows_of(i, n)
        for k in range(n):

            @pl.when(has_left)
            def _(k=k):
                halo_right(i + k).wait_recv()

            @pl.when(has_right)
            def _(k=k):
                halo_left(i + k).wait_recv()

        owned = []
        for k in range(n):
            kvg_s[i + k, HALO : 2 * HALO, :] += halo_recv[i + k, 0].astype(F32)
            kvg_s[i + k, length : length + HALO, :] += halo_recv[i + k, 1].astype(F32)
            owned.append(kvg_s[i + k, HALO : HALO + length, :].astype(BF16))
        dq = dq_s[at, :]
        add_vector("query_bias", col_sum(dq))
        grads = lanes(dq.astype(BF16), rows(*owned), glow_s[at, :])
        first = first_s[at, :]
        weight_grads = t_mm(first, grads[:, : 3 * width])
        for k, name in enumerate(GROUP_TWO[:3]):
            add2(name, weight_grads[:, k * width : (k + 1) * width])
        first_grad = mm_t(
            grads, lanes(query_weight[...], key_weight[...], value_weight[...], gate_weight[...])
        )
        scaling = sig_s[at, :]
        single_hat = shat_s[at, :]
        cond_hat = chat_s[at, :]
        scaled_grad = first_grad * scaling
        before = scaled_grad * single_hat * (1.0 - scaling)
        both = lanes(before.astype(BF16), first_grad.astype(BF16))
        low1 = (cond_hat * first_gain[...]).astype(BF16)
        both_grad = t_mm(low1, both)
        add2("first_scale", both_grad[:, :width])
        add2("first_shift", both_grad[:, width:])
        add_vector("first_lift", col_sum(before))
        cond_normed = mm_t(both, lanes(first_scale[...], first_shift[...]))
        add_vector("first_gain", col_sum(cond_normed * cond_hat))
        atom_grad = mid_grad_s[at, :] + normalize_back(single_hat, sinv_s[at, :], scaled_grad)
        agrad_o[pl.ds(i, n)] = atom_grad.reshape(n, length, width)
        cond_grad = cond_normed * first_gain[...] + cnorm_s[at, :]
        cond_grad = normalize_back(cond_hat, cinv_s[at, :], cond_grad) + cdir_s[at, :]
        cgrad_o[pl.ds(i, n)] = cond_grad.reshape(n, length, width)

    steps(FINISH_ITEMS, finish_rows)

    def pair_back(i):
        wide = widet_s[...]
        for w in range(0, windows, 2):
            both = lanes(dl_s[i, w], dl_s[i, w + 1])
            product = mm(wide, rows(both, both))
            for v in (0, 1):
                at = window_at(i, w + v)
                block = pair_rows(i, w + v).astype(F32)
                part = product[:, v * KW : (v + 1) * KW].reshape(channels, QW, KW)
                pgrad_o[i, :, (w + v) * QW : (w + v + 1) * QW, :] = (
                    part - (block - mean_s[at, :][None]) * t_s[at, :][None]
                )

    def pair_part(part):
        low, high = part * items // 4, (part + 1) * items // 4

        def step(i, carry):
            pair_back(i)
            return carry

        lax.fori_loop(low, high, step, 0)

    sum2.scatter()
    sum1.over_dp()
    pair_part(0)
    sum2.over_dp()
    pair_part(1)
    sum1.gather()
    pair_part(2)
    sum2.gather()
    pair_part(3)
    sum1.finish()
    sum2.finish()

    def drain(i, carry):
        @pl.when(has_right)
        def _():
            halo_right(i).wait_send()

        @pl.when(has_left)
        def _():
            halo_left(i).wait_send()

        return carry

    lax.fori_loop(0, items, drain, 0)


GRADS = (
    "first_gain",
    "first_scale",
    "first_lift",
    "first_shift",
    "query_weight",
    "query_bias",
    "key_weight",
    "value_weight",
    "gate_weight",
    "pair_gain",
    "pair_weight",
    "output_weight",
    "branch_gate",
    "branch_lift",
    "second_gain",
    "second_scale",
    "second_lift",
    "second_shift",
    "hidden_gate",
    "hidden_up",
    "hidden_down",
    "closing_gate",
    "closing_lift",
)
SPLIT = {
    "hidden_gate": ("hidden_gate_a", "hidden_gate_b"),
    "hidden_up": ("hidden_up_a", "hidden_up_b"),
}


def results_kernel(
    pgrad_in,
    layer_in,
    agrad_in,
    cgrad_in,
    red1,
    red2,
    pair_gain,
    pair_weight,
    pgrad_o,
    layer_o,
    agrad_o,
    cgrad_o,
    *rest,
):
    grads = dict(zip(GRADS, rest[: len(GRADS)]))
    (sem,) = rest[len(GRADS) :]
    copies = [
        pltpu.make_async_copy(src, dst, sem.at[k])
        for k, (src, dst) in enumerate(
            (
                (pgrad_in, pgrad_o),
                (agrad_in, agrad_o),
                (cgrad_in, cgrad_o),
                (layer_in, layer_o),
            )
        )
    ]
    for copy in copies:
        copy.start()
    width = red1.shape[1]

    def one(name):
        at = GROUP_ONE.index(name) * width
        return red1[at : at + width, :].astype(F32)

    vector_at = len(GROUP_TWO) * width
    tail = red2[vector_at : vector_at + 32, :].astype(F32)
    for name in GRADS:
        ref = grads[name]
        if name in SPLIT:
            for k, part in enumerate(SPLIT[name]):
                ref[:, k * width : (k + 1) * width] = one(part)
        elif name == "hidden_down":
            ref[0:width, :] = one("hidden_down_a")
            ref[width : 2 * width, :] = one("hidden_down_b")
        elif name in GROUP_ONE:
            ref[...] = one(name)
        elif name in GROUP_TWO:
            at = GROUP_TWO.index(name) * width
            ref[...] = red2[at : at + width, :].astype(F32)
        elif name in VECTORS:
            at = VECTORS.index(name)
            ref[...] = tail[at : at + 1, :]
    heads, channels = pair_weight.shape
    eye = jnp.where(iota((channels, channels), 0) == iota((channels, channels), 1), 1.0, 0.0)
    sums = tail[8 : 8 + channels, :]
    pick = jnp.where(iota((heads, width), 0) == iota((heads, width), 1), 1.0, 0.0)
    turned = mm_t(pick, sums, HIGHEST)
    grads["pair_weight"][...] = turned * pair_gain[...]
    grads["pair_gain"][...] = jnp.sum(pair_weight[...] * turned, axis=0, keepdims=True)
    for copy in copies:
        copy.wait()


def shards(
    n_a,
    n_d,
    atom_single,
    atom_cond,
    atom_pair,
    atom_counts,
    cotangent,
    *params,
):
    items, length, width = atom_single.shape
    windows = length // QW
    channels = atom_pair.shape[1]
    named = dict(zip(GRADS, params))
    named["pair_weight"] = named["pair_weight"].T
    flat = [v.reshape(1, -1) if v.ndim == 1 else v for v in named.values()]
    heads = named["pair_weight"].shape[0]
    hq, cq = heads * QW, channels * QW
    rows1 = len(GROUP_ONE) * width
    rows2 = len(GROUP_TWO) * width + 8 + channels
    shard1, shard2 = shard_rows(rows1, n_a), shard_rows(rows2, n_a)

    vmem = pl.BlockSpec(memory_space=pltpu.VMEM)
    anywhere = pl.BlockSpec(memory_space=pl.ANY)
    by_items = (items, length, width)
    by_rows = (items * length, width)
    by_keys = (items * length, KW)
    ext = length + 2 * HALO
    dma = pltpu.SemaphoreType.DMA

    def in_hbm(value):
        return pltpu.with_memory_space_constraint(value, pltpu.HBM)

    def sds(shape, dtype):
        return jax.ShapeDtypeStruct(shape, dtype)

    outs = pl.pallas_call(
        functools.partial(main_kernel, n_a, n_d),
        out_shape=[
            pltpu.VMEM(by_items, BF16),
            pltpu.VMEM(by_items, F32),
            pltpu.VMEM(by_items, F32),
            pltpu.VMEM((items, channels, length, KW), F32),
            pltpu.VMEM((n_a, shard1, width), BF16),
            pltpu.VMEM((n_a, shard2, width), BF16),
        ],
        in_specs=[pl.BlockSpec(memory_space=pltpu.SMEM), vmem, vmem, vmem, anywhere]
        + [vmem] * len(flat),
        out_specs=[vmem] * 6,
        scratch_shapes=[
            pltpu.VMEM((items, channels, length, KW), BF16),
            pltpu.VMEM((items, ext, 2 * width), BF16),
            pltpu.VMEM(by_rows, BF16),
            pltpu.VMEM(by_rows, BF16),
            pltpu.VMEM(by_rows, F32),
            pltpu.VMEM(by_rows, F32),
            pltpu.VMEM(by_rows, F32),
            pltpu.VMEM(by_rows, F32),
            pltpu.VMEM(by_rows, F32),
            pltpu.VMEM(by_rows, F32),
            pltpu.VMEM((items, windows, hq, KW), F32),
            pltpu.VMEM((items, windows, hq, KW), F32),
            pltpu.VMEM(by_keys, F32),
            pltpu.VMEM(by_keys, F32),
            pltpu.VMEM(by_rows, F32),
            pltpu.VMEM(by_rows, F32),
            pltpu.VMEM(by_rows, F32),
            pltpu.VMEM(by_rows, F32),
            pltpu.VMEM(by_rows, BF16),
            pltpu.VMEM(by_rows, BF16),
            pltpu.VMEM((items, windows, hq, KW), BF16),
            pltpu.VMEM(by_keys, F32),
            pltpu.VMEM(by_rows, F32),
            pltpu.VMEM((items, ext, 2 * width), F32),
            pltpu.VMEM((2 * hq, cq), BF16),
            pltpu.VMEM((cq, 2 * hq), BF16),
            pltpu.VMEM((hq, width), BF16),
            pltpu.VMEM((cq, hq), F32),
            pltpu.VMEM((n_a * shard1, width), F32),
            pltpu.VMEM((n_a * shard2, width), F32),
            pltpu.VMEM((items, 2, HALO, 2 * width), BF16),
            pltpu.VMEM((items, 2, HALO, 2 * width), BF16),
            pltpu.VMEM((n_a, shard1, width), BF16),
            pltpu.VMEM((n_a, shard1, width), BF16),
            pltpu.VMEM((n_d, shard1, width), BF16),
            pltpu.VMEM((n_a, shard2, width), BF16),
            pltpu.VMEM((n_a, shard2, width), BF16),
            pltpu.VMEM((n_d, shard2, width), BF16),
            dma((items,)),
            dma((2,)),
            dma((2,)),
            dma((items, 2)),
            dma((items, 2)),
            dma((n_a,)),
            dma((n_a,)),
            dma((n_d,)),
            dma((n_d,)),
            dma((n_a,)),
            dma((n_a,)),
            dma((n_a,)),
            dma((n_a,)),
            dma((n_d,)),
            dma((n_d,)),
            dma((n_a,)),
            dma((n_a,)),
        ],
        compiler_params=pltpu.CompilerParams(
            collective_id=0, has_side_effects=True, vmem_limit_bytes=44 * 1024 * 1024
        ),
        name="block",
    )(*[in_hbm(v) for v in (atom_counts, atom_single, atom_cond, cotangent, atom_pair, *flat)])
    layer, agrad, cgrad, pgrad, red1, red2 = outs
    red1 = red1.reshape(n_a * shard1, width)
    red2 = red2.reshape(n_a * shard2, width)
    grad_shapes = [
        (1, v.shape[0]) if v.ndim == 1 else v.shape for v in (named[name] for name in GRADS)
    ]
    finals = pl.pallas_call(
        results_kernel,
        out_shape=[
            sds(atom_pair.shape, F32),
            sds(by_items, BF16),
            sds(by_items, F32),
            sds(by_items, F32),
        ]
        + [sds(shape, F32) for shape in grad_shapes],
        in_specs=[anywhere] * 4 + [vmem] * 4,
        out_specs=[anywhere] * 4 + [vmem] * len(GRADS),
        scratch_shapes=[dma((4,))],
        compiler_params=pltpu.CompilerParams(vmem_limit_bytes=16 * 1024 * 1024),
        name="results",
    )(
        pgrad,
        layer,
        agrad,
        cgrad,
        red1,
        red2,
        in_hbm(named["pair_gain"].reshape(1, -1)),
        in_hbm(named["pair_weight"]),
    )
    pgrad, layer, agrad, cgrad, *weight_grads = finals
    weight_grads = [
        g.T if n == "pair_weight" else g.reshape(named[n].shape)
        for g, n in zip(weight_grads, GRADS)
    ]
    return (layer, agrad, pgrad, cgrad, *weight_grads)


def solution(mesh):
    atoms = P("dp", "atoms", None)
    pair = P("dp", None, "atoms", None)
    return jax.shard_map(
        functools.partial(shards, mesh.shape["atoms"], mesh.shape["dp"]),
        mesh=mesh,
        in_specs=(atoms, atoms, pair, P("dp"), atoms) + (P(),) * len(GRADS),
        out_specs=(atoms, atoms, pair, atoms) + (P(),) * len(GRADS),
        check_vma=False,
    )
```

time: 65.1 us -> 46.3 us (0.71)
  local copies, waits for them, and re-layouts: 12.6 us -> 0 us
  Pallas kernels: 51.3 us -> 45.4 us
    unnamed x26 -> x0, local copies, waits for them, and re-layouts: 12.6 us -> none
    pallas_call x2, Pallas kernels: 51.3 us -> 45.4 us  [the longest x1 39.8 us: shards(): pl.pallas_call(functools.partial(main_kernel, n_a, n_d), out_shape=[pltpu...]
where the time goes in v2:
time: 46.3 us; the launch traced here: 46.1 us
  Pallas kernels  45.4 us (98%)
  between operations  0.69 us (1%)
    pallas_call x1, Pallas kernels, shards(): pl.pallas_call(functools.partial(main_kernel, n_a, n_d), out_shape=[pltpu...  39.8 us
    pallas_call x1, Pallas kernels, shards(): pl.pallas_call(results_kernel, out_shape=[sds(atom_pair.shape, F32), sds(...  5.64 us

profile of v2, /device:TPU:0, one launch (start us, length us, event | category | flops | bytes accessed | tf_op | source)
XLA Modules:
  0.0 46.1 jit_solution(8283462148200091246)
XLA Ops:
  0.7 39.8 %block.1 = (bf16[4,256,128]{2,1,0:T(8,128)(2,1)S(1)}, f32[4,256,128]{2,1,0:T(8,128)S(1)}, f32[4,256,128]{2,1,0:T(8,128)S(1)}, f32[4,16,256,128]{3,2,1,0:T(8,128)...) custom-call(s32[4]{0:T(128)} %counts.1, bf16[4,256,128]{2,1,0:T(8,128)(2,1)} %single.1, ...), custom_call_target="tpu_custom_call" | custom-call | tf_op jit(solution)/shard_map/block/pallas_call | solution.py:937
  40.5 5.6 %results.1 = (f32[4,16,256,128]{3,2,1,0:T(8,128)}, bf16[4,256,128]{2,1,0:T(8,128)(2,1)}, f32[4,256,128]{2,1,0:T(8,128)}, f32[4,256,128]{2,1,0:T(8,128)}, f32[1,1...) custom-call(f32[4,16,256,128]{3,2,1,0:T(8,128)S(1)} %get-tuple-eleme, ...), custom_call_target="tpu_custom_call" | custom-call | tf_op jit(solution)/shard_map/results/pallas_call | solution.py:1018

commit v3 on v0

v3 whole, which is shorter than its diff:
```python
import functools
from typing import Any, NamedTuple

import jax
import jax.numpy as jnp
from jax import lax
from jax.experimental import pallas as pl
from jax.experimental.pallas import tpu as pltpu
from jax.sharding import PartitionSpec as P

QW = 32
KW = 128
HALO = 48
SPREAD = KW // QW
EPSILON = 1e-05
MASKED = -1000000000.0
HIGHEST = lax.Precision.HIGHEST
MESH = pl.DeviceIdType.MESH
F32 = jnp.float32
BF16 = jnp.bfloat16
PROJECT_START = 4
PAIR_START = 1
ATTEND_START = 16
MIDDLE_START = 4
BACK_START = 16
FINISH_START = 4

HIDDEN_GATE, HIDDEN_UP, HIDDEN_DOWN = (0, 0), (0, 2), (0, 4)
OUTPUT, BRANCH, CLOSING, SECOND_SCALE, SECOND_SHIFT, GATE = [(1, k) for k in range(6)]
QUERY, KEY, VALUE = [(2, k) for k in range(3)]
FIRST_SCALE, FIRST_SHIFT = [(3, k) for k in range(2)]
BLOCKS = (6, 6, 3, 2)
SUMS = len(BLOCKS)
(
    V_FIRST_GAIN,
    V_FIRST_LIFT,
    V_QUERY_BIAS,
    V_BRANCH_LIFT,
    V_SECOND_GAIN,
    V_SECOND_LIFT,
    V_CLOSING_LIFT,
) = range(7)
VECTOR_ROWS = 8


class Params(NamedTuple):
    first_gain: Any
    first_scale: Any
    first_lift: Any
    first_shift: Any
    query_weight: Any
    query_bias: Any
    key_weight: Any
    value_weight: Any
    gate_weight: Any
    pair_gain: Any
    pair_weight: Any
    output_weight: Any
    branch_gate: Any
    branch_lift: Any
    second_gain: Any
    second_scale: Any
    second_lift: Any
    second_shift: Any
    hidden_gate: Any
    hidden_up: Any
    hidden_down: Any
    closing_gate: Any
    closing_lift: Any


EARLY_PARAMS = 11


class Inputs(NamedTuple):
    counts: Any
    pair: Any
    single: Any
    cond: Any
    cot: Any


class Outputs(NamedTuple):
    layer: Any
    agrad: Any
    cgrad: Any
    pgrad: Any
    gain: Any
    weight: Any


class Scratch(NamedTuple):
    counts: Any
    single: Any
    cond: Any
    cot: Any
    pair: Any
    keys: Any
    keys_grad: Any
    query: Any
    first: Any
    attended_low: Any
    gate_low: Any
    cond_hat: Any
    cond_inv: Any
    single_hat: Any
    single_inv: Any
    scaling: Any
    gating: Any
    attended: Any
    mid_grad: Any
    cond_normed: Any
    cond_direct: Any
    row_grad: Any
    pair_inv: Any
    pair_mean: Any
    term: Any
    probs: Any
    slopes: Any
    wide: Any
    wide_turned: Any
    head_mask: Any
    pair_sums: Any
    halo_send: Any
    halo_recv: Any
    in_sem: Any
    pair_sem: Any
    kv_send: Any
    kv_recv: Any
    hg_send: Any
    hg_recv: Any
    rs_send: Any
    rs_recv: Any
    ag_send: Any
    ag_recv: Any
    z_send: Any
    z_recv: Any


class SumScratch(NamedTuple):
    acc: Any
    send: Any
    recv: Any
    zall: Any


def mm(a, b, precision=None):
    return lax.dot_general(
        a, b, (((1,), (0,)), ((), ())), precision=precision, preferred_element_type=F32
    )


def mm_t(a, b, precision=None):
    return lax.dot_general(
        a, b, (((1,), (1,)), ((), ())), precision=precision, preferred_element_type=F32
    )


def t_mm(a, b):
    return lax.dot_general(a, b, (((0,), (0,)), ((), ())), preferred_element_type=F32)


def sigmoid(v):
    return 0.5 * jnp.tanh(0.5 * v) + 0.5


def lane_mean(v):
    return jnp.mean(v, axis=-1, keepdims=True)


def normalize(v):
    centre = v - lane_mean(v)
    inverse = lax.rsqrt(lane_mean(centre * centre) + EPSILON)
    return centre * inverse, jnp.broadcast_to(inverse, v.shape)


def normalize_back(normed, inverse, grads):
    return inverse * (grads - lane_mean(grads) - normed * lane_mean(grads * normed))


def lanes(*parts):
    return jnp.concatenate(parts, axis=1)


def rows(*parts):
    return jnp.concatenate(parts, axis=0)


def col_sum(v):
    return jnp.sum(v, axis=0, keepdims=True)


def iota(shape, axis):
    return lax.broadcasted_iota(jnp.int32, shape, axis)


def shard_rows(total, peers):
    return -(-total // (16 * peers)) * 16


def weave(parts, start):
    waiting, active = list(parts), []
    while waiting or active:
        active, waiting = active + waiting[:start], waiting[start:]
        going = []
        for part in active:
            try:
                next(part)
                going.append(part)
            except StopIteration:
                pass
        active = going


class Sum:
    def __init__(self, k, n_a, n_d, bufs, red, v):
        self.n_a, self.n_d = n_a, n_d
        self.me, self.me_d = lax.axis_index("atoms"), lax.axis_index("dp")
        self.acc, self.send, self.recv, self.zall = bufs
        self.red = red
        self.rs_send, self.rs_recv = v.rs_send.at[k], v.rs_recv.at[k]
        self.z_send, self.z_recv = v.z_send.at[k], v.z_recv.at[k]
        self.ag_send, self.ag_recv = v.ag_send.at[k], v.ag_recv.at[k]
        self.shard = self.send.shape[1]
        self.written = set()

    def add(self, block, value):
        at = slice(block * value.shape[1], block * value.shape[1] + value.shape[0])
        if block in self.written:
            self.acc[at, :] += value
        else:
            self.written.add(block)
            self.acc[at, :] = value

    def scatter_copy(self, to, at):
        return pltpu.make_async_remote_copy(
            src_ref=self.send.at[to],
            dst_ref=self.recv.at[at],
            send_sem=self.rs_send.at[to],
            recv_sem=self.rs_recv.at[at],
            device_id={"atoms": to},
            device_id_type=MESH,
        )

    def dp_copy(self, to, at):
        return pltpu.make_async_remote_copy(
            src_ref=self.zall.at[self.me_d],
            dst_ref=self.zall.at[at],
            send_sem=self.z_send.at[to],
            recv_sem=self.z_recv.at[at],
            device_id={"dp": to},
            device_id_type=MESH,
        )

    def gather_copy(self, to, at):
        return pltpu.make_async_remote_copy(
            src_ref=self.red.at[self.me],
            dst_ref=self.red.at[at],
            send_sem=self.ag_send.at[to],
            recv_sem=self.ag_recv.at[at],
            device_id={"atoms": to},
            device_id_type=MESH,
        )

    def each_atoms(self, body):
        def go(k, carry):
            body(lax.rem(self.me + k, self.n_a))
            return carry

        lax.fori_loop(1, self.n_a, go, 0)

    def each_dp(self, body):
        def go(k, carry):
            body(lax.rem(self.me_d + k, self.n_d))
            return carry

        lax.fori_loop(1, self.n_d, go, 0)

    def scatter(self):
        self.send[...] = self.acc[...].astype(BF16).reshape(self.send.shape)
        self.each_atoms(lambda peer: self.scatter_copy(peer, self.me).start())

    def over_dp(self):
        start = pl.multiple_of(self.me * self.shard, 16)
        total = self.acc[pl.ds(start, self.shard), :]
        for k in range(1, self.n_a):
            peer = lax.rem(self.me + k, self.n_a)
            self.scatter_copy(peer, peer).wait_recv()
            total = total + self.recv[peer].astype(F32)
        self.zall[self.me_d] = total.astype(BF16)
        self.each_dp(lambda peer: self.dp_copy(peer, self.me_d).start())
        self.each_atoms(lambda peer: self.scatter_copy(peer, peer).wait_send())

    def gather(self):
        self.each_dp(lambda peer: self.dp_copy(peer, peer).wait_recv())
        total = self.zall[0].astype(F32)
        for d in range(1, self.n_d):
            total = total + self.zall[d].astype(F32)
        self.red[self.me] = total.astype(BF16)
        self.each_atoms(lambda peer: self.gather_copy(peer, self.me).start())
        self.each_dp(lambda peer: self.dp_copy(peer, peer).wait_send())

    def finish(self):
        self.each_atoms(lambda peer: self.gather_copy(peer, peer).wait_recv())
        self.each_atoms(lambda peer: self.gather_copy(peer, peer).wait_send())


def main_kernel(n_a, n_d, *refs):
    def take(kind):
        nonlocal refs
        count = len(kind._fields)
        head, refs = refs[:count], refs[count:]
        return kind(*head)

    ins, params_in, out = take(Inputs), take(Params), take(Outputs)
    reds, refs = refs[:SUMS], refs[SUMS:]
    v, w_ = take(Scratch), take(Params)
    sums = [Sum(k, n_a, n_d, take(SumScratch), reds[k], v) for k in range(SUMS)]
    hidden_sum, middle_sum, qkv_sum, first_sum = sums

    items, length, width = v.single.shape
    windows = length // QW
    heads, channels = w_.pair_weight.shape
    head_dim = width // heads
    factor = head_dim ** (-0.5)
    me = lax.axis_index("atoms")
    me_d = lax.axis_index("dp")
    anchor = me * length
    has_left = me > 0
    has_right = me < n_a - 1

    pairs = [(ins.single, v.single), (ins.cond, v.cond)] + list(zip(params_in, w_))
    pairs += [(ins.cot, v.cot), (ins.counts, v.counts)]
    loads = [pltpu.make_async_copy(a, b, v.in_sem.at[k]) for k, (a, b) in enumerate(pairs)]
    early, late = loads[: 2 + EARLY_PARAMS], loads[2 + EARLY_PARAMS :]

    def pair_copy(i):
        return pltpu.make_async_copy(ins.pair.at[i], v.pair.at[i], v.pair_sem.at[i])

    for load in early:
        load.start()
    for i in range(items):
        pair_copy(i).start()
    for load in late:
        load.start()

    v.keys[:, 0:HALO, :] = jnp.zeros((items, HALO, 2 * width), BF16)
    v.keys[:, HALO + length : 2 * HALO + length, :] = jnp.zeros((items, HALO, 2 * width), BF16)
    v.halo_recv[...] = jnp.zeros(v.halo_recv.shape, BF16)

    barrier = pltpu.get_barrier_semaphore()

    def greet(axis, peer):
        pl.semaphore_signal(barrier, inc=1, device_id={axis: peer}, device_id_type=MESH)

    hidden_sum.each_atoms(functools.partial(greet, "atoms"))
    hidden_sum.each_dp(functools.partial(greet, "dp"))

    hq = heads * QW
    cq = channels * QW
    v.head_mask[...] = jnp.where(
        iota((hq, width), 0) // QW == iota((hq, width), 1) // head_dim, 1.0, 0.0
    ).astype(BF16)
    pick_head = jnp.where(iota((hq, heads), 0) // QW == iota((hq, heads), 1), 1.0, 0.0)
    spread = jnp.where(iota((channels, cq), 0) == iota((channels, cq), 1) // QW, 1.0, 0.0).astype(
        BF16
    )
    same_row = iota((hq, cq), 0) % QW == iota((hq, cq), 1) % QW
    for group, count in zip(sums, BLOCKS):
        unused = slice(0 if group is first_sum else count * width, group.acc.shape[0])
        if unused.start < unused.stop:
            group.acc[unused, :] = jnp.zeros((unused.stop - unused.start, width), F32)
    v.pair_sums[...] = jnp.zeros(v.pair_sums.shape, F32)
    for load in early:
        load.wait()
    out.gain[...] = w_.pair_gain[...]
    out.weight[...] = w_.pair_weight[...]
    weighted = mm(pick_head, w_.pair_weight[...], HIGHEST) * w_.pair_gain[...]
    weighted = weighted - lane_mean(weighted)
    high = weighted.astype(BF16)
    low = (weighted - high.astype(F32)).astype(BF16)
    wide_high = jnp.where(same_row, mm(high, spread), 0.0)
    wide_low = jnp.where(same_row, mm(low, spread), 0.0)
    v.wide[0:hq, :] = wide_high.astype(BF16)
    v.wide[hq : 2 * hq, :] = wide_low.astype(BF16)
    v.wide_turned[:, 0:hq] = wide_high.T.astype(BF16)
    v.wide_turned[:, hq : 2 * hq] = wide_low.T.astype(BF16)

    def add(place, value):
        sums[place[0]].add(place[1], value)

    vectors_at = BLOCKS[-1] * width
    pair_at = vectors_at + VECTOR_ROWS

    def add_vector(k, value):
        first_sum.acc[vectors_at + k : vectors_at + k + 1, :] += value

    def rows_of(i):
        return slice(i * length, (i + 1) * length)

    def alive(i):
        place = anchor + iota((length, width), 0)
        return jnp.where(place < v.counts[i], 1.0, 0.0)

    def project(i):
        at = rows_of(i)
        cond_hat, cond_inv = normalize(v.cond[i].astype(F32))
        v.cond_hat[at, :] = cond_hat
        v.cond_inv[at, :] = cond_inv
        low1 = (cond_hat * w_.first_gain[...]).astype(BF16)
        yield
        pre = mm(low1, lanes(w_.first_scale[...], w_.first_shift[...]))
        single_hat, single_inv = normalize(v.single[i].astype(F32))
        v.single_hat[at, :] = single_hat
        v.single_inv[at, :] = single_inv
        yield
        scaling = sigmoid(pre[:, :width] + w_.first_lift[...])
        v.scaling[at, :] = scaling
        first = (scaling * single_hat + pre[:, width:]).astype(BF16)
        v.first[at, :] = first
        yield
        key_value = mm(first, lanes(w_.key_weight[...], w_.value_weight[...]))
        query_gate = mm(first, lanes(w_.query_weight[...], w_.gate_weight[...]))
        yield
        v.keys[i, HALO : HALO + length, :] = key_value.astype(BF16)
        v.query[at, :] = (query_gate[:, :width] + w_.query_bias[...]).astype(BF16)
        v.gating[at, :] = sigmoid(query_gate[:, width:])

    weave([project(i) for i in range(items)], PROJECT_START)

    pl.semaphore_wait(barrier, n_a - 1 + n_d - 1)
    right, left = lax.rem(me + 1, n_a), lax.rem(me + n_a - 1, n_a)

    def to_right(src, dst, send_sem, recv_sem):
        return pltpu.make_async_remote_copy(
            src, dst, send_sem, recv_sem, device_id={"atoms": right}, device_id_type=MESH
        )

    def to_left(src, dst, send_sem, recv_sem):
        return pltpu.make_async_remote_copy(
            src, dst, send_sem, recv_sem, device_id={"atoms": left}, device_id_type=MESH
        )

    kv_right = to_right(
        v.keys.at[:, pl.ds(length, HALO), :],
        v.keys.at[:, pl.ds(0, HALO), :],
        v.kv_send.at[0],
        v.kv_recv.at[0],
    )
    kv_left = to_left(
        v.keys.at[:, pl.ds(HALO, HALO), :],
        v.keys.at[:, pl.ds(HALO + length, HALO), :],
        v.kv_send.at[1],
        v.kv_recv.at[1],
    )

    def where_right(*actions):
        @pl.when(has_right)
        def _():
            for action in actions:
                action()

    def where_left(*actions):
        @pl.when(has_left)
        def _():
            for action in actions:
                action()

    where_right(kv_right.start)
    where_left(kv_left.start)

    def window_at(i, w):
        at = i * length + w * QW
        return slice(at, at + QW)

    def pair_rows(i, w):
        return v.pair[i, :, w * QW : (w + 1) * QW, :]

    def pair_forward(i, w):
        both = lanes(pair_rows(i, w).reshape(cq, KW), pair_rows(i, w + 1).reshape(cq, KW))
        product = mm(v.wide[...], both)
        invs = []
        for u in (w, w + 1):
            block = pair_rows(i, u).astype(F32)
            mean = jnp.mean(block, axis=0)
            centre = block - mean[None]
            inv = lax.rsqrt(jnp.mean(centre * centre, axis=0) + EPSILON)
            v.pair_mean[window_at(i, u), :] = mean
            v.pair_inv[window_at(i, u), :] = inv
            invs.append(inv)
        yield
        product = product[:hq] + product[hq:]
        for u in (0, 1):
            part = product[:, u * KW : (u + 1) * KW].reshape(heads, QW, KW)
            v.term[i, w + u] = (part * invs[u][None]).reshape(hq, KW)

    for i in range(items):
        pair_copy(i).wait()
        weave([pair_forward(i, w) for w in range(0, windows, 2)], PAIR_START)

    inner = [w for w in range(windows) if w * QW >= HALO and (w + 1) * QW + HALO <= length]
    outer = [w for w in range(windows) if w not in inner]

    def every(ws):
        return [(i, w) for i in range(items) for w in ws]

    def spread_heads(block):
        return rows(*([block] * heads)) * v.head_mask[...]

    def gather_heads(wide_block):
        lane = iota((QW, width), 1)
        result = wide_block[(heads - 1) * QW :]
        for h in range(heads - 2, -1, -1):
            result = jnp.where(
                lane < (h + 1) * head_dim, wide_block[h * QW : (h + 1) * QW], result
            )
        return result

    def keys_of(i, w):
        return v.keys[i, w * QW : w * QW + KW, 0:width]

    def values_of(i, w):
        return v.keys[i, w * QW : w * QW + KW, width : 2 * width]

    def attend(i, w):
        at = window_at(i, w)
        scores = mm_t(spread_heads(v.query[at, :]), keys_of(i, w))
        yield
        place = anchor + (w * QW - HALO) + iota((1, KW), 1)
        valid = (place >= 0) & (place < v.counts[i])
        logits = jnp.where(valid, scores * factor + v.term[i, w], MASKED)
        top = jnp.max(logits, axis=-1, keepdims=True)
        yield
        raised = jnp.exp(logits - top)
        total = jnp.sum(raised, axis=-1, keepdims=True)
        yield
        probs = raised * (1.0 / total)
        v.probs[i, w] = probs
        attended = mm(probs.astype(BF16), values_of(i, w))
        yield
        v.attended[at, :] = gather_heads(attended)

    for load in late:
        load.wait()
    weave([attend(*a) for a in every(inner)], ATTEND_START)
    where_left(kv_right.wait_recv)
    where_right(kv_left.wait_recv)
    weave([attend(*a) for a in every(outer)], ATTEND_START)
    where_right(kv_right.wait_send)
    where_left(kv_left.wait_send)

    def middle(i):
        at = rows_of(i)
        cond_rows = v.cond[i]
        att = v.attended[at, :]
        gating = v.gating[at, :]
        gated = (gating * att).astype(BF16)
        branch = mm(gated, w_.output_weight[...])
        zeros = mm(cond_rows, lanes(w_.branch_gate[...], w_.closing_gate[...]))
        low2 = (v.cond_hat[at, :] * w_.second_gain[...]).astype(BF16)
        pre = mm(low2, lanes(w_.second_scale[...], w_.second_shift[...]))
        yield
        live = alive(i)
        zero_one = sigmoid(zeros[:, :width] + w_.branch_lift[...])
        zero_two = sigmoid(zeros[:, width:] + w_.closing_lift[...])
        live_one = live * zero_one
        live_two = live * zero_two
        mid = v.single[i].astype(F32) + live_one * branch
        mid_hat, mid_inv = normalize(mid)
        scaling = sigmoid(pre[:, :width] + w_.second_lift[...])
        second = (scaling * mid_hat + pre[:, width:]).astype(BF16)
        yield
        pre = mm(second, lanes(w_.hidden_gate[...], w_.hidden_up[...]))
        half = pre.shape[1] // 2
        gate_pre, up_pre = pre[:, :half], pre[:, half:]
        yield
        gate_sig = sigmoid(gate_pre)
        gate_silu = gate_pre * gate_sig
        hidden = (gate_silu * up_pre).astype(BF16)
        out_grad = v.cot[i].astype(F32)
        closing_full = out_grad * live_two
        closing_grad = closing_full.astype(BF16)
        yield
        closing = mm(hidden, w_.hidden_down[...])
        hidden_grad = mm_t(closing_grad, w_.hidden_down[...])
        add(HIDDEN_DOWN, t_mm(hidden, closing_grad))
        yield
        gate_slope = gate_sig + gate_silu * (1.0 - gate_sig)
        gate_pre_grad = (hidden_grad * up_pre * gate_slope).astype(BF16)
        up_pre_grad = (hidden_grad * gate_silu).astype(BF16)
        gate_up_grad = lanes(gate_pre_grad, up_pre_grad)
        yield
        second_grad = mm_t(gate_up_grad, lanes(w_.hidden_gate[...], w_.hidden_up[...]))
        wide_grad = t_mm(second, gate_up_grad)
        for k in range(4):
            add((0, k), wide_grad[:, k * width : (k + 1) * width])
        out.layer[i] = (mid + live_two * closing).astype(BF16)
        zero_two_pre = closing_full * closing * (1.0 - zero_two)
        add_vector(V_CLOSING_LIFT, col_sum(zero_two_pre))
        if i == items - 1:
            hidden_sum.scatter()
        yield
        scaled_grad = second_grad * scaling
        mid_grad = out_grad + normalize_back(mid_hat, mid_inv, scaled_grad)
        v.mid_grad[at, :] = mid_grad
        branch_full = mid_grad * live_one
        branch_grad = branch_full.astype(BF16)
        yield
        attended_grad = mm_t(branch_grad, w_.output_weight[...]) * gating
        v.attended_low[at, :] = attended_grad.astype(BF16)
        add(OUTPUT, t_mm(gated, branch_grad))
        before = scaled_grad * mid_hat * (1.0 - scaling)
        both = lanes(before.astype(BF16), second_grad.astype(BF16))
        add_vector(V_SECOND_LIFT, col_sum(before))
        both_grad = t_mm(low2, both)
        add(SECOND_SCALE, both_grad[:, :width])
        add(SECOND_SHIFT, both_grad[:, width:])
        cond_normed = mm_t(both, lanes(w_.second_scale[...], w_.second_shift[...]))
        yield
        gate_low = (attended_grad * att * (1.0 - gating)).astype(BF16)
        v.gate_low[at, :] = gate_low
        zero_one_pre = branch_full * branch * (1.0 - zero_one)
        add_vector(V_BRANCH_LIFT, col_sum(zero_one_pre))
        zero_grads = lanes(zero_one_pre.astype(BF16), zero_two_pre.astype(BF16))
        add(GATE, t_mm(v.first[at, :], gate_low))
        gate_grads = t_mm(cond_rows, zero_grads)
        add(BRANCH, gate_grads[:, :width])
        add(CLOSING, gate_grads[:, width:])
        v.cond_direct[at, :] = mm_t(zero_grads, lanes(w_.branch_gate[...], w_.closing_gate[...]))
        add_vector(V_SECOND_GAIN, col_sum(cond_normed * v.cond_hat[at, :]))
        v.cond_normed[at, :] = cond_normed * w_.second_gain[...]

    weave([middle(i) for i in range(items)], MIDDLE_START)

    def halo_right(i):
        return to_right(
            v.halo_send.at[i, 1], v.halo_recv.at[i, 0], v.hg_send.at[i, 1], v.hg_recv.at[i, 0]
        )

    def halo_left(i):
        return to_left(
            v.halo_send.at[i, 0], v.halo_recv.at[i, 1], v.hg_send.at[i, 0], v.hg_recv.at[i, 1]
        )

    folded = {}

    def attend_back(i, w):
        at = window_at(i, w)
        wide_grad = spread_heads(v.attended_low[at, :])
        probs_grad = mm_t(wide_grad, values_of(i, w))
        probs = v.probs[i, w]
        value_grad = t_mm(probs.astype(BF16), wide_grad)
        yield
        inner_sum = jnp.sum(probs_grad * probs, axis=-1, keepdims=True)
        yield
        logits_grad = probs * (probs_grad - inner_sum)
        low = logits_grad.astype(BF16)
        by_head = logits_grad.reshape(heads, QW, KW)
        v.slopes[i, w] = (by_head * v.pair_inv[at, :][None]).astype(BF16).reshape(hq, KW)
        v.probs[i, w] = logits_grad
        query_grad = mm(low, keys_of(i, w))
        key_grad = t_mm(low, spread_heads(v.query[at, :]))
        yield
        v.row_grad[at, :] = gather_heads(query_grad) * factor
        for k in range(SPREAD):
            piece = slice(k * QW, (k + 1) * QW)
            piece = (key_grad[piece], value_grad[piece])
            if (i, w + k) in folded:
                piece = [a + b for a, b in zip(folded[i, w + k], piece)]
            folded[i, w + k] = piece

    def fold(i, blocks):
        for b in blocks:
            key_grad, value_grad = folded.pop((i, b))
            v.keys_grad[i, b * QW : (b + 1) * QW, :width] = key_grad * factor
            v.keys_grad[i, b * QW : (b + 1) * QW, width:] = value_grad

    blocks = range(windows + SPREAD - 1)
    ends = -(-HALO // QW)
    weave([attend_back(*a) for a in every(outer)], BACK_START)
    for i in range(items):
        for side, at in ((0, blocks[:ends]), (1, blocks[-ends:])):
            for k in (0, 1):
                edge = rows(*[folded[i, b][k] for b in at])
                edge = edge[:HALO] if side == 0 else edge[-HALO:]
                if k == 0:
                    edge = edge * factor
                v.halo_send[i, side, :, k * width : (k + 1) * width] = edge.astype(BF16)
    where_right(*[halo_right(i).start for i in range(items)])
    where_left(*[halo_left(i).start for i in range(items)])
    middle_sum.scatter()
    weave([attend_back(*a) for a in every(inner)], BACK_START)
    for i in range(items):
        fold(i, blocks)
    for i in range(items):
        if i == items // 2:
            hidden_sum.over_dp()
        pair_all = lanes(*[pair_rows(i, w).reshape(cq, KW) for w in range(windows)])
        slopes_all = lanes(*[v.slopes[i, w] for w in range(windows)])
        for k in (0, 1):
            half = slice(k * cq // 2, (k + 1) * cq // 2)
            v.pair_sums[half, :] += mm_t(pair_all[half], slopes_all)

    diagonal = jnp.where(iota((cq, hq), 0) % QW == iota((cq, hq), 1) % QW, v.pair_sums[...], 0.0)
    by_channel = jnp.sum(diagonal.reshape(channels, QW, hq), axis=1)
    gather = jnp.where(iota((hq, width), 0) // QW == iota((hq, width), 1), 1.0, 0.0)
    channel_sums = mm(by_channel, gather, HIGHEST)
    first_sum.acc[pair_at : pair_at + channels, :] = channel_sums - jnp.mean(
        channel_sums, axis=0, keepdims=True
    )

    where_left(*[halo_right(i).wait_recv for i in range(items)])
    where_right(*[halo_left(i).wait_recv for i in range(items)])

    def finish_rows(i):
        at = rows_of(i)
        v.keys_grad[i, HALO : 2 * HALO, :] += v.halo_recv[i, 0].astype(F32)
        v.keys_grad[i, length : length + HALO, :] += v.halo_recv[i, 1].astype(F32)
        query_grad = v.row_grad[at, :]
        add_vector(V_QUERY_BIAS, col_sum(query_grad))
        key_value = v.keys_grad[i, HALO : HALO + length, :].astype(BF16)
        grads = lanes(query_grad.astype(BF16), key_value, v.gate_low[at, :])
        yield
        weight_grads = t_mm(v.first[at, :], grads[:, : 3 * width])
        for k in range(3):
            add((2, k), weight_grads[:, k * width : (k + 1) * width])
        if i == items - 1:
            qkv_sum.scatter()
        first_grad = mm_t(
            grads,
            lanes(
                w_.query_weight[...],
                w_.key_weight[...],
                w_.value_weight[...],
                w_.gate_weight[...],
            ),
        )
        yield
        scaling = v.scaling[at, :]
        scaled_grad = first_grad * scaling
        before = scaled_grad * v.single_hat[at, :] * (1.0 - scaling)
        both = lanes(before.astype(BF16), first_grad.astype(BF16))
        add_vector(V_FIRST_LIFT, col_sum(before))
        v.row_grad[at, :] = scaled_grad
        yield
        cond_hat = v.cond_hat[at, :]
        low1 = (cond_hat * w_.first_gain[...]).astype(BF16)
        both_grad = t_mm(low1, both)
        add(FIRST_SCALE, both_grad[:, :width])
        add(FIRST_SHIFT, both_grad[:, width:])
        cond_normed = mm_t(both, lanes(w_.first_scale[...], w_.first_shift[...]))
        add_vector(V_FIRST_GAIN, col_sum(cond_normed * cond_hat))
        v.cond_normed[at, :] += cond_normed * w_.first_gain[...]

    weave([finish_rows(i) for i in range(items)], FINISH_START)

    def close_rows(i):
        at = rows_of(i)
        atom_grad = normalize_back(v.single_hat[at, :], v.single_inv[at, :], v.row_grad[at, :])
        out.agrad[i] = v.mid_grad[at, :] + atom_grad
        cond_grad = normalize_back(v.cond_hat[at, :], v.cond_inv[at, :], v.cond_normed[at, :])
        out.cgrad[i] = cond_grad + v.cond_direct[at, :]

    def pair_back(i):
        wide = v.wide_turned[...]
        for w in range(0, windows, 2):
            both = lanes(v.slopes[i, w], v.slopes[i, w + 1])
            both = rows(both, both)
            half = cq // 2
            product = rows(mm(wide[:half], both), mm(wide[half:], both))
            for u in (0, 1):
                at = window_at(i, w + u)
                grad = v.probs[i, w + u] * v.term[i, w + u]
                dot = jnp.sum(grad.reshape(heads, QW, KW), axis=0)
                inv = v.pair_inv[at, :]
                slope = dot * inv * inv * (1.0 / channels)
                block = pair_rows(i, w + u).astype(F32)
                part = product[:, u * KW : (u + 1) * KW].reshape(channels, QW, KW)
                out.pgrad[i, :, (w + u) * QW : (w + u + 1) * QW, :] = (
                    part - (block - v.pair_mean[at, :][None]) * slope[None]
                )

    def close_part(part):
        for i in range(part * items // 4, (part + 1) * items // 4):
            close_rows(i)
            pair_back(i)

    first_sum.scatter()
    close_part(0)
    middle_sum.over_dp()
    close_part(1)
    close_part(2)
    hidden_sum.gather()
    qkv_sum.over_dp()
    first_sum.over_dp()
    close_part(3)
    where_right(*[halo_right(i).wait_send for i in range(items)])
    where_left(*[halo_left(i).wait_send for i in range(items)])
    middle_sum.gather()
    qkv_sum.gather()
    first_sum.gather()
    for group in sums:
        group.finish()


def results_kernel(*refs):
    ins = Outputs(*refs[:6])
    reds, refs = refs[6 : 6 + SUMS], refs[6 + SUMS :]
    (pgrad, layer, agrad, cgrad), refs = refs[:4], refs[4:]
    count = len(Params._fields)
    grads, stages = Params(*refs[:count]), refs[count : count + SUMS]
    vectors, weight_s, gain_s, sem = refs[count + SUMS :]
    copies = []

    def send(src, dst):
        copy = pltpu.make_async_copy(src, dst, sem.at[len(copies)])
        copy.start()
        copies.append(copy)

    send(ins.pgrad, pgrad)
    send(ins.agrad, agrad)
    send(ins.cgrad, cgrad)
    send(ins.layer, layer)
    for stage, red in zip(stages, reds):
        stage[...] = red[...].astype(F32)
    width = layer.shape[-1]

    def block(place, n=1):
        return stages[place[0]].at[pl.ds(place[1] * width, n * width), :]

    for place, ref in (
        (OUTPUT, grads.output_weight),
        (BRANCH, grads.branch_gate),
        (CLOSING, grads.closing_gate),
        (SECOND_SCALE, grads.second_scale),
        (SECOND_SHIFT, grads.second_shift),
        (GATE, grads.gate_weight),
        (QUERY, grads.query_weight),
        (KEY, grads.key_weight),
        (VALUE, grads.value_weight),
        (FIRST_SCALE, grads.first_scale),
        (FIRST_SHIFT, grads.first_shift),
    ):
        send(block(place), ref)
    send(block(HIDDEN_DOWN, 2), grads.hidden_down)
    for place, ref in ((HIDDEN_GATE, grads.hidden_gate), (HIDDEN_UP, grads.hidden_up)):
        for k in (0, 1):
            send(block((place[0], place[1] + k)), ref.at[:, pl.ds(k * width, width)])
    tail = stages[-1]
    vectors_at = BLOCKS[-1] * width
    for k, ref in (
        (V_FIRST_GAIN, grads.first_gain),
        (V_FIRST_LIFT, grads.first_lift),
        (V_QUERY_BIAS, grads.query_bias),
        (V_BRANCH_LIFT, grads.branch_lift),
        (V_SECOND_GAIN, grads.second_gain),
        (V_SECOND_LIFT, grads.second_lift),
        (V_CLOSING_LIFT, grads.closing_lift),
    ):
        vectors[k] = tail[vectors_at + k : vectors_at + k + 1, :]
        send(vectors.at[k], ref)
    heads, channels = ins.weight.shape
    pair_at = vectors_at + VECTOR_ROWS
    pick = jnp.where(iota((heads, width), 0) == iota((heads, width), 1), 1.0, 0.0)
    turned = mm_t(pick, tail[pair_at : pair_at + channels, :], HIGHEST)
    weight_s[...] = turned * ins.gain[...]
    gain_s[...] = jnp.sum(ins.weight[...] * turned, axis=0, keepdims=True)
    send(weight_s, grads.pair_weight)
    send(gain_s, grads.pair_gain)
    for copy in copies:
        copy.wait()


def shards(n_a, n_d, single, cond, pair, counts, cot, *params):
    items, length, width = single.shape
    windows = length // QW
    channels = pair.shape[1]
    params = Params(*params)
    flat = Params(
        *[p.reshape(1, -1) if p.ndim == 1 else p for p in params._replace(pair_weight=params.pair_weight.T)]
    )
    heads = flat.pair_weight.shape[0]
    hq, cq = heads * QW, channels * QW
    totals = [count * width for count in BLOCKS]
    totals[-1] += VECTOR_ROWS + channels
    shard = [shard_rows(total, n_a) for total in totals]

    vmem = pl.BlockSpec(memory_space=pltpu.VMEM)
    anywhere = pl.BlockSpec(memory_space=pl.ANY)
    by_items = (items, length, width)
    ext = length + 2 * HALO
    dma = pltpu.SemaphoreType.DMA

    def f32(*shape):
        return pltpu.VMEM(shape, F32)

    def bf16(*shape):
        return pltpu.VMEM(shape, BF16)

    by_rows = f32(items * length, width)
    by_rows_low = bf16(items * length, width)
    by_keys = f32(items * length, KW)
    by_window = f32(items, windows, hq, KW)
    scratch = Scratch(
        counts=pltpu.SMEM(counts.shape, counts.dtype),
        single=bf16(*by_items),
        cond=bf16(*by_items),
        cot=bf16(*by_items),
        pair=bf16(*pair.shape),
        keys=bf16(items, ext, 2 * width),
        keys_grad=f32(items, ext, 2 * width),
        query=by_rows_low,
        first=by_rows_low,
        attended_low=by_rows_low,
        gate_low=by_rows_low,
        cond_hat=by_rows,
        cond_inv=by_rows,
        single_hat=by_rows,
        single_inv=by_rows,
        scaling=by_rows,
        gating=by_rows,
        attended=by_rows,
        mid_grad=by_rows,
        cond_normed=by_rows,
        cond_direct=by_rows,
        row_grad=by_rows,
        pair_inv=by_keys,
        pair_mean=by_keys,
        term=by_window,
        probs=by_window,
        slopes=bf16(items, windows, hq, KW),
        wide=bf16(2 * hq, cq),
        wide_turned=bf16(cq, 2 * hq),
        head_mask=bf16(hq, width),
        pair_sums=f32(cq, hq),
        halo_send=bf16(items, 2, HALO, 2 * width),
        halo_recv=bf16(items, 2, HALO, 2 * width),
        in_sem=dma((4 + len(params),)),
        pair_sem=dma((items,)),
        kv_send=dma((2,)),
        kv_recv=dma((2,)),
        hg_send=dma((items, 2)),
        hg_recv=dma((items, 2)),
        rs_send=dma((SUMS, n_a)),
        rs_recv=dma((SUMS, n_a)),
        ag_send=dma((SUMS, n_a)),
        ag_recv=dma((SUMS, n_a)),
        z_send=dma((SUMS, n_d)),
        z_recv=dma((SUMS, n_d)),
    )
    sum_scratch = [
        SumScratch(
            acc=f32(n_a * size, width),
            send=bf16(n_a, size, width),
            recv=bf16(n_a, size, width),
            zall=bf16(n_d, size, width),
        )
        for size in shard
    ]

    def in_hbm(value):
        return pltpu.with_memory_space_constraint(value, pltpu.HBM)

    outs = pl.pallas_call(
        functools.partial(main_kernel, n_a, n_d),
        out_shape=[
            *Outputs(
                layer=bf16(*by_items),
                agrad=f32(*by_items),
                cgrad=f32(*by_items),
                pgrad=f32(*pair.shape),
                gain=f32(1, channels),
                weight=f32(heads, channels),
            ),
            *[bf16(n_a, size, width) for size in shard],
        ],
        in_specs=[anywhere] * (5 + len(params)),
        out_specs=[vmem] * (6 + SUMS),
        scratch_shapes=[
            *scratch,
            *[pltpu.VMEM(p.shape, p.dtype) for p in flat],
            *[buf for bufs in sum_scratch for buf in bufs],
        ],
        compiler_params=pltpu.CompilerParams(
            collective_id=0, has_side_effects=True, vmem_limit_bytes=48 * 1024 * 1024
        ),
        name="block",
    )(*[in_hbm(x) for x in (counts, pair, single, cond, cot, *flat)])
    kept = Outputs(*outs[:6])
    reds = [red.reshape(-1, width) for red in outs[6:]]

    def sds(shape, dtype):
        return jax.ShapeDtypeStruct(shape, dtype)

    pgrad, layer, agrad, cgrad, *grads = pl.pallas_call(
        results_kernel,
        out_shape=[
            sds(pair.shape, F32),
            sds(by_items, BF16),
            sds(by_items, F32),
            sds(by_items, F32),
            *[sds(p.shape, F32) for p in flat],
        ],
        in_specs=[anywhere] * 4 + [vmem] * (2 + SUMS),
        out_specs=[anywhere] * (4 + len(params)),
        scratch_shapes=[
            *[f32(n_a * size, width) for size in shard],
            f32(VECTOR_ROWS, 1, width),
            f32(heads, channels),
            f32(1, channels),
            dma((6 + len(params),)),
        ],
        compiler_params=pltpu.CompilerParams(vmem_limit_bytes=16 * 1024 * 1024),
        name="results",
    )(*kept, *reds)
    grads = Params(*grads)
    grads = grads._replace(pair_weight=grads.pair_weight.T)
    return (layer, agrad, pgrad, cgrad, *[g.reshape(p.shape) for g, p in zip(grads, params)])


def solution(mesh):
    atoms = P("dp", "atoms", None)
    pair = P("dp", None, "atoms", None)
    count = len(Params._fields)
    return jax.shard_map(
        functools.partial(shards, mesh.shape["atoms"], mesh.shape["dp"]),
        mesh=mesh,
        in_specs=(atoms, atoms, pair, P("dp"), atoms) + (P(),) * count,
        out_specs=(atoms, atoms, pair, atoms) + (P(),) * count,
        check_vma=False,
    )
```

time: 385 us -> 38.7 us (0.10); the launches traced: 379 us -> 38.5 us
  waiting for transfers between devices: 130 us -> 0 us
  matrix products: 80.7 us -> 0 us
  local copies, waits for them, and re-layouts: 79.7 us -> 0 us
  other arithmetic: 61.7 us -> 0 us
  Pallas kernels: 0 us -> 37.7 us
  between operations: 15.7 us -> 0.85 us
  starting transfers between devices: 11.1 us -> 0 us
    psum x1 -> x0, waiting for transfers between devices: 130 us -> none  [shards(): flattened = lax.psum(flattened, ('dp', 'atoms'))]
    dot_general x42 -> x0, matrix products: 80.7 us -> none  [the longest x1 21.5 us: shards(): jnp.einsum('ihak,ch->icak', term_grad, pair_weight, precision=highest)]
    pallas_call x0 -> x2, Pallas kernels: none -> 37.7 us  [the longest x1 33.3 us: shards(): pl.pallas_call(functools.partial(main_kernel, n_a, n_d), out_shape=[*Outp...]
    concatenate x3 -> x0, local copies, waits for them, and re-layouts: 27.1 us -> none  [the longest x1 26.3 us: shards(): flattened = jnp.concatenate([member.reshape(-1) for member in weight_grads])]
    sub x2 -> x0, other arithmetic: 23.2 us -> none  [the longest x1 23.2 us: shards(): logits_grad = jnp.where(mask_full, probs * (probs_grad - row_inner), 0.0)]
    reshape x12 -> x0, local copies, waits for them, and re-layouts: 19 us -> none  [the longest x5 5.44 us: split_flat(): summed.append(flattened[offset:offset + extent].reshape(member.shape))]
    reduce_sum x9 -> x0, other arithmetic: 18.3 us -> none  [the longest x3 8.07 us: normalize(): centre = values - jnp.mean(values, axis=axis, keepdims=True)]
    unnamed x192 -> x0, local copies, waits for them, and re-layouts: 13.7 us -> none
  transfers between devices with their start and end apart: 5 -> 0, of which waited for: 1 -> 0; matrix products, arithmetic and copies ran while one was open for 22% -> 0% of each run, Pallas kernels for 0% -> 0%
where the time goes in v3:
time: 38.7 us; the launch traced here: 38.5 us
  Pallas kernels  37.7 us (97%)
  between operations  0.85 us (2%)
    pallas_call x1, Pallas kernels, shards(): pl.pallas_call(functools.partial(main_kernel, n_a, n_d), out_shape=[*Outp...  33.3 us
    pallas_call x1, Pallas kernels, shards(): pl.pallas_call(results_kernel, out_shape=[sds(pair.shape, F32), sds(by_it...  4.4 us

profile of v3, /device:TPU:0, one launch (start us, length us, event | category | flops | bytes accessed | tf_op | source)
XLA Modules:
  0.0 38.5 jit_solution(12636753161735328651)
XLA Ops:
  0.7 33.3 %block.1 = (bf16[4,256,128]{2,1,0:T(8,128)(2,1)S(1)}, f32[4,256,128]{2,1,0:T(8,128)S(1)}, f32[4,256,128]{2,1,0:T(8,128)S(1)}, f32[4,16,256,128]{3,2,1,0:T(8,128)...) custom-call(s32[4]{0:T(128)} %refs_0_.1, ...), custom_call_target="tpu_custom_call" | custom-call | tf_op jit(solution)/shard_map/block/pallas_call | solution.py:964
  34.0 4.4 %results.1 = (f32[4,16,256,128]{3,2,1,0:T(8,128)}, bf16[4,256,128]{2,1,0:T(8,128)(2,1)}, f32[4,256,128]{2,1,0:T(8,128)}, f32[4,256,128]{2,1,0:T(8,128)}, f32[1,1...) custom-call(bf16[4,256,128]{2,1,0:T(8,128)(2,1)S(1)} %get-tuple-elem, ...), custom_call_target="tpu_custom_call" | custom-call | tf_op jit(solution)/shard_map/results/pallas_call | solution.py:995

commit v4 on v3

--- a/solution.py
+++ b/solution.py
@@ -21,7 +21,7 @@
 PROJECT_START = 4
 PAIR_START = 1
 ATTEND_START = 16
-MIDDLE_START = 4
+MIDDLE_STEPS = 9
 BACK_START = 16
 FINISH_START = 4
 
@@ -608,6 +608,7 @@
         yield
         attended_grad = mm_t(branch_grad, w_.output_weight[...]) * gating
         v.attended_low[at, :] = attended_grad.astype(BF16)
+        yield
         add(OUTPUT, t_mm(gated, branch_grad))
         before = scaled_grad * mid_hat * (1.0 - scaling)
         both = lanes(before.astype(BF16), second_grad.astype(BF16))
@@ -630,7 +631,10 @@
         add_vector(V_SECOND_GAIN, col_sum(cond_normed * v.cond_hat[at, :]))
         v.cond_normed[at, :] = cond_normed * w_.second_gain[...]
 
-    weave([middle(i) for i in range(items)], MIDDLE_START)
+    middles = [middle(i) for i in range(items)]
+    for _ in range(MIDDLE_STEPS):
+        for part in middles:
+            next(part)
 
     def halo_right(i):
         return to_right(
@@ -677,19 +681,21 @@
 
     blocks = range(windows + SPREAD - 1)
     ends = -(-HALO // QW)
-    weave([attend_back(*a) for a in every(outer)], BACK_START)
-    for i in range(items):
-        for side, at in ((0, blocks[:ends]), (1, blocks[-ends:])):
-            for k in (0, 1):
-                edge = rows(*[folded[i, b][k] for b in at])
-                edge = edge[:HALO] if side == 0 else edge[-HALO:]
-                if k == 0:
-                    edge = edge * factor
-                v.halo_send[i, side, :, k * width : (k + 1) * width] = edge.astype(BF16)
-    where_right(*[halo_right(i).start for i in range(items)])
-    where_left(*[halo_left(i).start for i in range(items)])
+    for group in (range(items // 2), range(items // 2, items)):
+        weave([attend_back(i, w) for i in group for w in outer], BACK_START)
+        for i in group:
+            for side, at in ((0, blocks[:ends]), (1, blocks[-ends:])):
+                for k in (0, 1):
+                    edge = rows(*[folded[i, b][k] for b in at])
+                    edge = edge[:HALO] if side == 0 else edge[-HALO:]
+                    if k == 0:
+                        edge = edge * factor
+                    v.halo_send[i, side, :, k * width : (k + 1) * width] = edge.astype(BF16)
+        where_right(*[halo_right(i).start for i in group])
+        where_left(*[halo_left(i).start for i in group])
+    weave([attend_back(*a) for a in every(inner)], BACK_START)
+    weave(middles, items)
     middle_sum.scatter()
-    weave([attend_back(*a) for a in every(inner)], BACK_START)
     for i in range(items):
         fold(i, blocks)
     for i in range(items):
@@ -709,22 +715,25 @@
         channel_sums, axis=0, keepdims=True
     )
 
-    where_left(*[halo_right(i).wait_recv for i in range(items)])
-    where_right(*[halo_left(i).wait_recv for i in range(items)])
-
-    def finish_rows(i):
-        at = rows_of(i)
-        v.keys_grad[i, HALO : 2 * HALO, :] += v.halo_recv[i, 0].astype(F32)
-        v.keys_grad[i, length : length + HALO, :] += v.halo_recv[i, 1].astype(F32)
-        query_grad = v.row_grad[at, :]
+    def finish_rows(parts, last):
+        def read(ref):
+            return rows(*[ref[i * length + a : i * length + b, :] for i, a, b in parts])
+
+        def write(ref, value):
+            done = 0
+            for i, a, b in parts:
+                ref[i * length + a : i * length + b, :] = value[done : done + b - a]
+                done += b - a
+
+        query_grad = read(v.row_grad)
         add_vector(V_QUERY_BIAS, col_sum(query_grad))
-        key_value = v.keys_grad[i, HALO : HALO + length, :].astype(BF16)
-        grads = lanes(query_grad.astype(BF16), key_value, v.gate_low[at, :])
-        yield
-        weight_grads = t_mm(v.first[at, :], grads[:, : 3 * width])
+        key_value = rows(*[v.keys_grad[i, HALO + a : HALO + b, :] for i, a, b in parts])
+        grads = lanes(query_grad.astype(BF16), key_value.astype(BF16), read(v.gate_low))
+        yield
+        weight_grads = t_mm(read(v.first), grads[:, : 3 * width])
         for k in range(3):
             add((2, k), weight_grads[:, k * width : (k + 1) * width])
-        if i == items - 1:
+        if last:
             qkv_sum.scatter()
         first_grad = mm_t(
             grads,
@@ -736,23 +745,33 @@
             ),
         )
         yield
-        scaling = v.scaling[at, :]
+        scaling = read(v.scaling)
         scaled_grad = first_grad * scaling
-        before = scaled_grad * v.single_hat[at, :] * (1.0 - scaling)
+        before = scaled_grad * read(v.single_hat) * (1.0 - scaling)
         both = lanes(before.astype(BF16), first_grad.astype(BF16))
         add_vector(V_FIRST_LIFT, col_sum(before))
-        v.row_grad[at, :] = scaled_grad
-        yield
-        cond_hat = v.cond_hat[at, :]
+        write(v.row_grad, scaled_grad)
+        yield
+        cond_hat = read(v.cond_hat)
         low1 = (cond_hat * w_.first_gain[...]).astype(BF16)
         both_grad = t_mm(low1, both)
         add(FIRST_SCALE, both_grad[:, :width])
         add(FIRST_SHIFT, both_grad[:, width:])
         cond_normed = mm_t(both, lanes(w_.first_scale[...], w_.first_shift[...]))
         add_vector(V_FIRST_GAIN, col_sum(cond_normed * cond_hat))
-        v.cond_normed[at, :] += cond_normed * w_.first_gain[...]
-
-    weave([finish_rows(i) for i in range(items)], FINISH_START)
+        write(v.cond_normed, read(v.cond_normed) + cond_normed * w_.first_gain[...])
+
+    weave(
+        [finish_rows([(i, HALO, length - HALO)], False) for i in range(items)], FINISH_START
+    )
+    where_left(*[halo_right(i).wait_recv for i in range(items)])
+    where_right(*[halo_left(i).wait_recv for i in range(items)])
+    rim = []
+    for i in range(items):
+        v.keys_grad[i, HALO : 2 * HALO, :] += v.halo_recv[i, 0].astype(F32)
+        v.keys_grad[i, length : length + HALO, :] += v.halo_recv[i, 1].astype(F32)
+        rim += [(i, 0, HALO), (i, length - HALO, length)]
+    weave([finish_rows(rim, True)], FINISH_START)
 
     def close_rows(i):
         at = rows_of(i)

time: 38.7 us -> 38.5 us (level)
  no operation moved by 1% of the time
where the time goes in v4:
time: 38.5 us; the launch traced here: 38.3 us
  Pallas kernels  37.4 us (97%)
  between operations  0.85 us (2%)
    pallas_call x1, Pallas kernels, shards(): pl.pallas_call(functools.partial(main_kernel, n_a, n_d), out_shape=[*Outp...  33.1 us
    pallas_call x1, Pallas kernels, shards(): pl.pallas_call(results_kernel, out_shape=[sds(pair.shape, F32), sds(by_it...  4.4 us

profile of v4, /device:TPU:0, one launch (start us, length us, event | category | flops | bytes accessed | tf_op | source)
XLA Modules:
  0.0 38.3 jit_solution(12720672292244105958)
XLA Ops:
  0.7 33.1 %block.1 = (bf16[4,256,128]{2,1,0:T(8,128)(2,1)S(1)}, f32[4,256,128]{2,1,0:T(8,128)S(1)}, f32[4,256,128]{2,1,0:T(8,128)S(1)}, f32[4,16,256,128]{3,2,1,0:T(8,128)...) custom-call(s32[4]{0:T(128)} %refs_0_.1, ...), custom_call_target="tpu_custom_call" | custom-call | tf_op jit(solution)/shard_map/block/pallas_call | solution.py:983
  33.7 4.4 %results.1 = (f32[4,16,256,128]{3,2,1,0:T(8,128)}, bf16[4,256,128]{2,1,0:T(8,128)(2,1)}, f32[4,256,128]{2,1,0:T(8,128)}, f32[4,256,128]{2,1,0:T(8,128)}, f32[1,1...) custom-call(bf16[4,256,128]{2,1,0:T(8,128)(2,1)S(1)} %get-tuple-elem, ...), custom_call_target="tpu_custom_call" | custom-call | tf_op jit(solution)/shard_map/results/pallas_call | solution.py:1014

commit v5 on v4

--- a/solution.py
+++ b/solution.py
@@ -24,6 +24,7 @@
 MIDDLE_STEPS = 9
 BACK_START = 16
 FINISH_START = 4
+UNROLLED = 8
 
 HIDDEN_GATE, HIDDEN_UP, HIDDEN_DOWN = (0, 0), (0, 2), (0, 4)
 OUTPUT, BRANCH, CLOSING, SECOND_SCALE, SECOND_SHIFT, GATE = [(1, k) for k in range(6)]
@@ -262,19 +263,23 @@
             device_id_type=MESH,
         )
 
+    def each(self, me, count, body):
+        if count <= UNROLLED:
+            for k in range(1, count):
+                body(lax.rem(me + k, count))
+            return
+
+        def go(k, carry):
+            body(lax.rem(me + k, count))
+            return carry
+
+        lax.fori_loop(1, count, go, 0)
+
     def each_atoms(self, body):
-        def go(k, carry):
-            body(lax.rem(self.me + k, self.n_a))
-            return carry
-
-        lax.fori_loop(1, self.n_a, go, 0)
+        self.each(self.me, self.n_a, body)
 
     def each_dp(self, body):
-        def go(k, carry):
-            body(lax.rem(self.me_d + k, self.n_d))
-            return carry
-
-        lax.fori_loop(1, self.n_d, go, 0)
+        self.each(self.me_d, self.n_d, body)
 
     def scatter(self):
         self.send[...] = self.acc[...].astype(BF16).reshape(self.send.shape)

time: 38.5 us -> 38.5 us (level)
  no operation moved by 1% of the time
where the time goes in v5:
time: 38.5 us; the launch traced here: 38.3 us
  Pallas kernels  37.5 us (97%)
  between operations  0.85 us (2%)
    pallas_call x1, Pallas kernels, shards(): pl.pallas_call(functools.partial(main_kernel, n_a, n_d), out_shape=[*Outp...  33.1 us
    pallas_call x1, Pallas kernels, shards(): pl.pallas_call(results_kernel, out_shape=[sds(pair.shape, F32), sds(by_it...  4.4 us

profile of v5, /device:TPU:0, one launch (start us, length us, event | category | flops | bytes accessed | tf_op | source)
XLA Modules:
  0.0 38.3 jit_solution(11786727549878578605)
XLA Ops:
  0.7 33.1 %block.1 = (bf16[4,256,128]{2,1,0:T(8,128)(2,1)S(1)}, f32[4,256,128]{2,1,0:T(8,128)S(1)}, f32[4,256,128]{2,1,0:T(8,128)S(1)}, f32[4,16,256,128]{3,2,1,0:T(8,128)...) custom-call(s32[4]{0:T(128)} %refs_0_.1, ...), custom_call_target="tpu_custom_call" | custom-call | tf_op jit(solution)/shard_map/block/pallas_call | solution.py:988
  33.7 4.4 %results.1 = (f32[4,16,256,128]{3,2,1,0:T(8,128)}, bf16[4,256,128]{2,1,0:T(8,128)(2,1)}, f32[4,256,128]{2,1,0:T(8,128)}, f32[4,256,128]{2,1,0:T(8,128)}, f32[1,1...) custom-call(bf16[4,256,128]{2,1,0:T(8,128)(2,1)S(1)} %get-tuple-elem, ...), custom_call_target="tpu_custom_call" | custom-call | tf_op jit(solution)/shard_map/results/pallas_call | solution.py:1019
